TPU v7x, 256 devices: a whole 4x4x8 slice. The times are simulated.
256 devices in a mesh: dp: 32 (over z, x_lo, core), tensor: 8 (over y, x_hi).
Axes of the slice: x: 4 (x_hi: 2, x_lo: 2; x = x_hi * 2 + x_lo), y: 4, z: 8, core: 2. Of those that a mesh axis runs over, the one named last changes fastest.
Arguments:
- inputs: bfloat16 [32768, 5120], P(('dp', 'tensor')), may hold values from -36 to 36
- norm_gain: bfloat16 [5120], replicated, may hold values from 0.099609375 to 1.8984375
- key_weight: bfloat16 [5120, 1024], P('dp', 'tensor'), may hold values from -0.078125 to 0.078125
- value_weight: bfloat16 [5120, 1024], P('dp', 'tensor'), may hold values from -0.078125 to 0.078125
- head_gain: bfloat16 [128], replicated, may hold values from 0.099609375 to 1.8984375
- key_cotangent: bfloat16 [32768, 1024], P('dp', 'tensor'), may hold values from -6 to 6
- value_cotangent: bfloat16 [32768, 1024], P('dp', 'tensor'), may hold values from -6 to 6
Outputs:
- key_states: bfloat16 [32768, 1024], P('dp', 'tensor')
- value_states: bfloat16 [32768, 1024], P('dp', 'tensor')
- input_grad: bfloat16 [32768, 5120], P(('dp', 'tensor'))
- key_weight_grad: float32 [5120, 1024], P('dp', 'tensor')
- value_weight_grad: float32 [5120, 1024], P('dp', 'tensor')
- norm_gain_grad: float32 [5120], replicated
- head_gain_grad: float32 [128], replicated
All inputs are finite; a program needn't handle non-finite values.
Results may differ from a plain program's by a relative error of at most 0.005.
Values may be sent and summed in bfloat16 or wider, within the bound.
A program may use at most 128 MiB of HBM per device.

v0:
```python
import jax
import jax.numpy as jnp
from jax import lax
from jax.sharding import PartitionSpec as P

eps = 1e-06


def on_device(
    inputs, norm_gain, key_weight, value_weight, head_gain, key_cotangent, value_cotangent
):
    xf = inputs.astype(jnp.float32)
    rinv = lax.rsqrt(jnp.mean(xf * xf, axis=-1, keepdims=True) + eps)
    normed = xf * rinv
    gain_in = norm_gain.astype(jnp.float32)
    hidden = (normed * gain_in).astype(jnp.bfloat16)
    group = lax.all_gather(hidden, "tensor", axis=0, tiled=True)
    key_full, value_full = (
        lax.all_gather(key_weight, "dp", axis=0, tiled=True),
        lax.all_gather(value_weight, "dp", axis=0, tiled=True),
    )
    key_raw = jnp.dot(group, key_full, preferred_element_type=jnp.float32)
    value_states = jnp.dot(group, value_full, preferred_element_type=jnp.float32).astype(
        jnp.bfloat16
    )
    group_rows = group.shape[0]
    width = key_raw.shape[1]
    head_size = head_gain.shape[0]
    heads = key_raw.reshape(group_rows, width // head_size, head_size)
    krinv = lax.rsqrt(jnp.mean(heads * heads, axis=-1, keepdims=True) + eps)
    key_normed = heads * krinv
    gain_head = head_gain.astype(jnp.float32)
    key_states = (key_normed * gain_head).reshape(group_rows, width).astype(jnp.bfloat16)
    cot_heads = key_cotangent.astype(jnp.float32).reshape(group_rows, width // head_size, head_size)
    key_back = cot_heads * gain_head
    key_raw_grad = krinv * (
        key_back - key_normed * jnp.mean(key_back * key_normed, axis=-1, keepdims=True)
    )
    key_raw_grad = key_raw_grad.reshape(group_rows, width).astype(jnp.bfloat16)
    head_part = jnp.sum(cot_heads * key_normed, axis=(0, 1))
    both_cot = jnp.concatenate([key_raw_grad, value_cotangent], axis=1)
    grads = lax.psum_scatter(
        lax.dot_general(
            group, both_cot, (((0,), (0,)), ((), ())), preferred_element_type=jnp.float32
        ),
        "dp",
        scatter_dimension=0,
        tiled=True,
    )
    key_weight_grad = grads[:, :width]
    value_weight_grad = grads[:, width:]
    both_weights = jnp.concatenate([key_full, value_full], axis=1)
    hidden_grad = lax.psum_scatter(
        lax.dot_general(
            both_cot, both_weights, (((1,), (1,)), ((), ())), preferred_element_type=jnp.float32
        ),
        "tensor",
        scatter_dimension=0,
        tiled=True,
    )
    norm_part = jnp.sum(hidden_grad * normed, axis=0)
    back = hidden_grad * gain_in
    input_grad = (rinv * (back - normed * jnp.mean(back * normed, axis=-1, keepdims=True))).astype(
        jnp.bfloat16
    )
    norm_gain_grad, head_gain_grad = lax.psum((norm_part, head_part), ("dp", "tensor"))
    return (
        key_states,
        value_states,
        input_grad,
        key_weight_grad,
        value_weight_grad,
        norm_gain_grad,
        head_gain_grad,
    )


def solution(mesh):
    in_specs = (
        P(("dp", "tensor"), None),
        P(),
        P("dp", "tensor"),
        P("dp", "tensor"),
        P(),
        P("dp", "tensor"),
        P("dp", "tensor"),
    )
    out_specs = (
        P("dp", "tensor"),
        P("dp", "tensor"),
        P(("dp", "tensor"), None),
        P("dp", "tensor"),
        P("dp", "tensor"),
        P(),
        P(),
    )
    return jax.shard_map(
        on_device, mesh=mesh, in_specs=in_specs, out_specs=out_specs, check_vma=False
    )
```

profile of v0, /device:TPU:16, one launch (start us, length us, event | category | flops | bytes accessed | tf_op | source)
XLA Modules:
  0.0 722.8 jit_solution(7723324745515766260)
XLA Ops:
  7.2 0.0 all-gather.6.cloned.1.call-start
  7.2 0.7 all-gather.6.cloned.1.call-update
  7.9 0.0 all-gather.4.cloned.1.call-start
  7.9 0.7 convert_element_type.28
  8.7 0.0 copy-start.6
  8.7 0.0 copy-start.4
  8.7 0.0 copy-start.5
  8.7 1.7 fusion.10
  10.4 2.8 fusion.4
  13.2 0.0 all-gather.4.cloned.1.call-update
  13.2 0.0 all-gather.8.cloned.1.call-start
  13.2 0.7 all-gather.8.cloned.1.call-update
  13.9 0.0 reduce-scatter.5.cloned.1.call-start
  14.0 0.0 copy-done.6
  14.0 0.0 copy-done.4
  14.0 0.1 copy.14
  14.2 0.0 copy-done.5
  14.2 0.1 copy.15
  14.3 62.5 %all-gather.6.cloned.1.call-done = bf16[5120,128]{1,0:T(8,128)(2,1)} async-done(((bf16[160,128]{1,0:T(8,128)(2,1)}), bf16[5120,128]{1,0:T(8,128)(2,1)}) %all-gather.6.cloned.1.call-update) | async-done | bytes 1310736 | tf_op jit(solution)/shard_map/all_gather | solution.py:19
  76.8 132.3 %all-gather.4.cloned.1.call-done = bf16[1024,5120]{1,0:T(8,128)(2,1)} async-done(((bf16[128,5120]{1,0:T(8,128)(2,1)}), bf16[1024,5120]{1,0:T(8,128)(2,1)}) %all-gather.4.cloned.1.call-update) | async-done | bytes 10485776 | tf_op jit(solution)/shard_map/all_gather | solution.py:17
  209.1 0.0 copy-start.1
  209.1 8.0 %multiply_reduce_fusion = (f32[1024]{0:T(1024)S(1)}, f32[1024,128]{0,1:T(8,128)S(1)}) fusion(bf16[1024,5120]{1,0:T(8,128)(2,1)} %all-gather.4.cloned.1.call-done, bf16[5120,128]{1,0:T(8,128)(2,1)} %all-gather.6.cloned.1.call-done), kind=kOutput, calls=%fused_computation.28 | convolution fusion | flops 1342438400 | bytes 12324864 | tf_op jit(solution)/shard_map/dot_general | solution.py:22
  217.2 0.2 fusion.20
  217.4 0.2 fusion.19
  217.6 0.0 copy-done.1
  217.6 4.8 fusion.21
  222.5 0.0 copy-start.2
  222.5 0.0 reduce-scatter.5.cloned.1.call-update
  222.5 0.0 reduce-scatter.3.cloned.1.call-start
  222.5 52.1 %all-gather.8.cloned.1.call-done = bf16[5120,128]{1,0:T(8,128)(2,1)} async-done(((bf16[160,128]{1,0:T(8,128)(2,1)}), bf16[5120,128]{1,0:T(8,128)(2,1)}) %all-gather.8.cloned.1.call-update) | async-done | bytes 1310736 | tf_op jit(solution)/shard_map/all_gather | solution.py:20
  274.6 0.0 copy-done.2
  274.6 9.9 %fusion.11 = f32[1024,5120]{1,0:T(8,128)} fusion(bf16[5120,128]{1,0:T(8,128)(2,1)} %all-gather.8.cloned.1.call-done, bf16[5120,128]{1,0:T(8,128)(2,1)S(1)} %copy-done.2, bf16[1024,128]{0,1:T(8,128)(2,1)S(1)} %copy.15, bf16[1024,128]{0,1:T(8,128)(2,1)S(1)} %get-tuple-element.20), kind=kOutput, calls=%fused_computation.13 | convolution fusion | flops 2690646016 | bytes 24117248 | tf_op jit(solution)/shard_map/dot_general | solution.py:54
  284.5 0.0 copy-start.3
  284.5 0.0 reduce-scatter.3.cloned.1.call-update
  284.5 0.8 copy.16
  285.4 0.5 copy-done.3
  285.9 0.0 copy-start
  285.9 6.5 convolution_convert_fusion
  292.4 109.1 %reduce-scatter.5.cloned.1.call-done = f32[160,256]{1,0:T(8,128)} async-done(((f32[5120,256]{1,0:T(8,128)}), f32[160,256]{1,0:T(8,128)}) %reduce-scatter.5.cloned.1.call-update) | async-done | bytes 163856 | tf_op jit(solution)/shard_map/reduce_scatter | solution.py:42
  401.5 1.6 fusion.24
  403.1 230.8 %reduce-scatter.3.cloned.1.call-done = f32[128,5120]{1,0:T(8,128)} async-done(((f32[1024,5120]{1,0:T(8,128)}), f32[128,5120]{1,0:T(8,128)}) %reduce-scatter.3.cloned.1.call-update) | async-done | bytes 2621456 | tf_op jit(solution)/shard_map/reduce_scatter | solution.py:53
  633.9 0.0 copy-done
  633.9 2.6 fusion.9
  636.6 76.2 %all-reduce = (f32[5120]{0:T(1024)}, f32[128]{0:T(128)}) all-reduce(f32[5120]{0:T(1024)S(1)} %get-tuple-element.14, f32[128]{0:T(128)S(1)} %get-tuple-element.16), channel_id=1, replica_groups=mesh['dp'=32,'tensor'=8] {'dp','tensor'}, use_global_device_ids=true, to_apply=%region_7.0 | all-reduce | flops 5248 | bytes 41984 | tf_op jit(solution)/shard_map/psum | solution.py:66
  712.8 3.5 fusion.8
  (5 shorter events, 0.0 us)
Async XLA Ops:
  7.2 69.6 %all-gather.6.cloned.1.call-start = ((), (), s32[]{:S(2)}) async-start(), calls=%async_computation.3 | async-start | bytes 1351680 | tf_op jit(solution)/shard_map/all_gather | solution.py:19
  7.9 201.2 %all-gather.4.cloned.1.call-start = ((), (), s32[]{:S(2)}) async-start(), calls=%async_computation.2 | async-start | bytes 11796480 | tf_op jit(solution)/shard_map/all_gather | solution.py:17
  8.7 5.3 copy-start.6
  8.7 5.3 copy-start.4
  8.7 5.5 copy-start.5
  13.2 261.4 %all-gather.8.cloned.1.call-start = ((), (), s32[]{:S(2)}) async-start(), calls=%async_computation.4 | async-start | bytes 1351680 | tf_op jit(solution)/shard_map/all_gather | solution.py:20
  13.9 387.6 %reduce-scatter.5.cloned.1.call-start = ((), (), s32[]{:S(2)}) async-start(), calls=%async_computation.6 | async-start | bytes 5406720 | tf_op jit(solution)/shard_map/reduce_scatter | solution.py:42
  209.1 8.5 %copy-start.1 = (bf16[1024,5120]{1,0:T(8,128)(2,1)S(1)}, bf16[1024,5120]{1,0:T(8,128)(2,1)}, u32[]{:S(2)}) copy-start(bf16[1024,5120]{1,0:T(8,128)(2,1)} %all-gather.4.cloned.1.call-done) | copy-start | bytes 31457284
  222.5 52.2 %copy-start.2 = (bf16[5120,128]{1,0:T(8,128)(2,1)S(1)}, bf16[5120,128]{1,0:T(8,128)(2,1)}, u32[]{:S(2)}) copy-start(bf16[5120,128]{1,0:T(8,128)(2,1)} %all-gather.6.cloned.1.call-done) | copy-start | bytes 3932164
  222.5 411.4 %reduce-scatter.3.cloned.1.call-start = ((), (), s32[]{:S(2)}) async-start(), calls=%async_computation.5 | async-start | bytes 23592960 | tf_op jit(solution)/shard_map/reduce_scatter | solution.py:53
  284.5 1.4 copy-start.3
  285.9 348.0 %copy-start = (bf16[128,5120]{1,0:T(8,128)(2,1)S(1)}, bf16[128,5120]{1,0:T(8,128)(2,1)}, u32[]{:S(2)}) copy-start(bf16[128,5120]{1,0:T(8,128)(2,1)} %param.7) | copy-start | bytes 3932164
Sparse Core Ops, SparseCore 0:
  9.9 66.8 all-gather.5
  79.9 129.1 all-gather.3
  211.0 63.5 all-gather.7
  277.0 124.4 reduce-scatter.4
  405.6 228.2 reduce-scatter.2
where the time goes:
time: 725 us; the launch traced here: 723 us
  waiting for transfers between devices  588 us (81%)
  blocking collectives  76.2 us (11%)
  matrix products  29.3 us (4%)
  between operations  13.9 us (2%)
  other arithmetic  11.7 us (2%)
    reduce_scatter x1, waiting for transfers between devices, on_device(): lax.psum_scatter(lax.dot_general(both_cot, both_weights, (((1,), (1,)), (...  231 us
    all_gather x1, waiting for transfers between devices, on_device(): group = lax.all_gather(hidden, 'tensor', axis=0, tiled=True)  132 us
    reduce_scatter x1, waiting for transfers between devices, on_device(): lax.psum_scatter(lax.dot_general(group, both_cot, (((0,), (0,)), ((), ())...  109 us
    psum x1, blocking collectives, on_device(): lax.psum((norm_part, head_part), ('dp', 'tensor'))  76.2 us
    all_gather x1, waiting for transfers between devices, on_device(): lax.all_gather(key_weight, 'dp', axis=0, tiled=True)  62.5 us
    all_gather x1, waiting for transfers between devices, on_device(): lax.all_gather(value_weight, 'dp', axis=0, tiled=True)  52.1 us
  transfers between devices with their start and end apart: 5, of which 5 were waited for; matrix products, arithmetic and copies ran while one was open for 5% of the time, Pallas kernels for 0%

commit v1 on v0

v1 whole, which is shorter than its diff:
```python
import jax
import jax.numpy as jnp
from jax import lax
from jax.experimental import pallas as pl
from jax.experimental.pallas import tpu as pltpu
from jax.sharding import PartitionSpec as P

eps = 1e-06
MESH = pl.DeviceIdType.MESH
T = 128
D = 5120
DC = 1280
R = 160
H = 128
bf16 = jnp.bfloat16
f32 = jnp.float32


def dot(a, b):
    return jnp.dot(a, b, preferred_element_type=f32)


def dot_nt(a, b):
    return lax.dot_general(a, b, (((1,), (1,)), ((), ())), preferred_element_type=f32)


def loop(n, body):
    def step(i, carry):
        body(i)
        return carry

    lax.fori_loop(0, n, step, 0)


def kernel(
    x_ref,
    gain_ref,
    wk_ref,
    wv_ref,
    hgain_ref,
    kcot_ref,
    vcot_ref,
    ks_ref,
    vs_ref,
    ig_ref,
    dwk_ref,
    dwv_ref,
    ng_ref,
    hg_ref,
    hid,
    hc,
    hct,
    w,
    psend,
    precv,
    own,
    cot,
    cb,
    oown,
    orecv,
    dhv,
    dhs,
    dhr,
    dw,
    dwc,
    dwx,
    zs,
    zr,
    fin,
    finr,
    vx,
    vz,
    vc,
    vy,
    rinv_s,
    s_w0,
    s_wz,
    s_wx,
    s_wc,
    s_hid,
    s_cot,
    s_va,
    s_ka,
    s_p,
    s_out,
    s_dh,
    s_dc,
    s_dx,
    s_dz,
    s_dp,
    s_vx,
    s_vz,
    s_vc,
    s_vy,
):
    dp, tn = lax.axis_index("dp"), lax.axis_index("tensor")
    z, xl, c = lax.div(dp, 4), lax.rem(lax.div(dp, 2), 2), lax.rem(dp, 2)
    y, xh = lax.div(tn, 2), lax.rem(tn, 2)
    x = 2 * xh + xl
    zh, ze = lax.div(z, 2), lax.rem(z, 2)

    def device(x, y, z, c):
        return (z * 4 + lax.rem(x, 2) * 2 + c, y * 2 + lax.div(x, 2))

    def ring_x(d):
        return lax.rem(x + d, 4)

    def ring_y(d):
        return lax.rem(y + d, 4)

    def ring_z(d):
        return lax.rem(z + d, 8)

    def at_x(px):
        return device(px, y, z, c)

    def at_y(py):
        return device(x, py, z, c)

    def at_z(pz):
        return device(x, y, pz, c)

    core = device(x, y, z, 1 - c)
    opposite = device(2 * (1 - xh) + xl, y, z, c)
    partner = device(x, zh, 2 * y + ze, c)
    moved = zh != y

    def send(src, dst, sems, s_at, r_at, to):
        pltpu.make_async_remote_copy(
            src_ref=src,
            dst_ref=dst,
            send_sem=sems.at[(0,) + s_at],
            recv_sem=sems.at[(1,) + r_at],
            device_id=to,
            device_id_type=MESH,
        ).start()

    def copy_of(ref, sems, at):
        return pltpu.make_async_remote_copy(
            src_ref=ref,
            dst_ref=ref,
            send_sem=sems.at[(0,) + at],
            recv_sem=sems.at[(1,) + at],
            device_id=core,
            device_id_type=MESH,
        )

    def arrived(ref, sems, at):
        copy_of(ref, sems, at).wait_recv()

    def sent(ref, sems, at):
        copy_of(ref, sems, at).wait_send()

    barrier = pltpu.get_barrier_semaphore()

    def hello(to):
        pl.semaphore_signal(barrier, inc=1, device_id=to, device_id_type=MESH)

    for d in range(1, 4):
        hello(at_x(ring_x(d)))
        hello(at_y(ring_y(d)))
    for d in range(1, 8):
        hello(at_z(ring_z(d)))
    hello(core)

    @pl.when(moved)
    def _():
        hello(partner)

    def norm_rows(i):
        rows = pl.ds(pl.multiple_of(i * 16, 16), 16)
        xf = x_ref[rows, :].astype(f32)
        rinv = lax.rsqrt(jnp.mean(xf * xf, axis=-1, keepdims=True) + eps)
        rinv_s[rows, :] = jnp.broadcast_to(rinv, (16, 128))
        hd = (xf * rinv * gain_ref[...]).astype(bf16)
        for k in range(4):
            hid[k, rows, :] = hd[:, k * DC : (k + 1) * DC]

    loop(8, norm_rows)
    hc[y] = hid[y]
    cb[1, y, xh] = vcot_ref[:, xh]
    cot[xh] = kcot_ref[:, xh]

    pl.semaphore_wait(barrier, jnp.where(moved, 15, 14))

    def w_own(kv):
        return w.at[kv, zh, xh, ze, xl, c]

    @pl.when(moved)
    def _():
        for kv, ref in ((0, wk_ref), (1, wv_ref)):
            send(ref, w.at[kv, y, xh, ze, xl, c], s_w0, (kv,), (kv,), partner)

    @pl.when(jnp.logical_not(moved))
    def _():
        for kv, ref in ((0, wk_ref), (1, wv_ref)):
            w[kv, zh, xh, ze, xl, c] = ref[...]

    for d in (1, 3, 2):
        py = ring_y(d)
        send(hid.at[py], hc.at[y], s_hid, (py,), (y,), at_y(py))
    send(vcot_ref.at[:, 1 - xh], cb.at[1, y, xh], s_cot, (1,), (1,), opposite)
    send(kcot_ref.at[:, 1 - xh], cot.at[xh], s_cot, (0,), (0,), opposite)

    def z_sends(kv):
        @pl.when(moved)
        def _():
            arrived(w_own(kv), s_w0, (kv,))

        def body(i):
            pz = ring_z(i + 1)
            send(w_own(kv), w_own(kv), s_wz, (kv, pz), (kv, z), at_z(pz))

        loop(7, body)

    def x_sends(kv, i):
        h = ring_y(i + 1)

        def wait_z(e):
            pz = 2 * h + e

            @pl.when(pz != z)
            def _():
                arrived(w.at[kv, h, xh, e, xl, c], s_wz, (kv, pz))

        loop(2, wait_z)
        part = w.at[kv, h, xh, :, xl, c]
        for d in (1, 3, 2):
            px = ring_x(d)
            send(part, part, s_wx, (kv, h, px), (kv, h, x), at_x(px))

    def core_sends(kv, i):
        h = ring_y(i + 1)

        def wait_x(d):
            px = ring_x(d + 1)
            pxl, pxh = lax.rem(px, 2), lax.div(px, 2)
            arrived(w.at[kv, h, pxh, :, pxl, c], s_wx, (kv, h, px))

        loop(3, wait_x)
        part = w.at[kv, h, :, :, :, c]
        send(part, part, s_wc, (kv, h), (kv, h), core)

    z_sends(0)
    z_sends(1)
    arrived(cb.at[1, y, 1 - xh], s_cot, (1,))
    for d in (1, 3, 2):
        py = ring_y(d)
        send(cb.at[1, y], cb.at[1, y], s_va, (py,), (y,), at_y(py))
    loop(4, lambda i: x_sends(0, i))

    def panel(kv, h):
        return jnp.concatenate(
            [w[kv, h, 0].reshape(DC, H), w[kv, h, 1].reshape(DC, H)], axis=1
        )

    def tokens():
        return hc[...].reshape(4 * T, DC)

    def forward(kv, i):
        h = ring_y(i + 1)
        arrived(w.at[kv, h, :, :, :, 1 - c], s_wc, (kv, h))
        part = dot(tokens(), panel(kv, h))

        @pl.when(h != y)
        def _():
            psend[kv, h] = part.astype(bf16)

        @pl.when(h == y)
        def _():
            own[kv] = part

    def partial_send(kv, d):
        py = ring_y(d)
        send(psend.at[kv, py], precv.at[kv, y], s_p, (kv, py), (kv, y), at_y(py))

    def hidden_wait(d):
        py = ring_y(d + 1)
        arrived(hc.at[py], s_hid, (py,))

    loop(3, hidden_wait)

    def key_step(i):
        @pl.when(i < 4)
        def _():
            core_sends(0, i)
            x_sends(1, i)

        @pl.when(i > 0)
        def _():
            forward(0, i - 1)

        @pl.when(jnp.logical_and(i > 0, i < 4))
        def _():
            partial_send(0, i)

    loop(5, key_step)

    for k in range(4):
        hct[:, k * T : (k + 1) * T] = hc[k].T

    def grad_tile(kv, h):
        ct = jnp.concatenate(
            [cb[kv, h, 0].reshape(4 * T, H), cb[kv, h, 1].reshape(4 * T, H)], axis=1
        )
        g = dot(hct[...], ct).astype(bf16).reshape(2, 2, 2, R, 2 * H)
        for pc in range(2):
            for ph in range(2):
                for pxl in range(2):
                    dw[kv, h, pc, 2 * ph + pxl] = g[:, pxl, pc, :, ph * H : (ph + 1) * H]
        send(dw.at[kv, h, 1 - c], dwc.at[kv, h], s_dc, (kv, h), (kv, h), core)

    def grad_core(kv, h):
        arrived(dwc.at[kv, h], s_dc, (kv, h))
        dw[kv, h, c] = (dw[kv, h, c].astype(f32) + dwc[kv, h].astype(f32)).astype(bf16)
        for d in (1, 3, 2):
            px = ring_x(d)
            send(
                dw.at[kv, h, c, px], dwx.at[kv, h, x], s_dx, (kv, h, px), (kv, h, x), at_x(px)
            )

    def grad_x(kv, h):
        total = dw[kv, h, c, x].astype(f32)
        for d in range(1, 4):
            px = ring_x(d)
            arrived(dwx.at[kv, h, px], s_dx, (kv, h, px))
            total = total + dwx[kv, h, px].astype(f32)
        zs[kv, h] = total.astype(bf16)

        def body(e):
            pz = 2 * h + e

            @pl.when(pz != z)
            def _():
                send(zs.at[kv, h, e], zr.at[kv, z], s_dz, (kv, pz), (kv, z), at_z(pz))

        loop(2, body)

    def grad_z(kv):
        total = zs[kv, zh, ze].astype(f32)
        for d in range(1, 8):
            pz = ring_z(d)
            arrived(zr.at[kv, pz], s_dz, (kv, pz))
            total = total + zr[kv, pz].astype(f32)

        @pl.when(moved)
        def _():
            fin[kv] = total
            send(fin.at[kv], finr.at[kv], s_dp, (kv,), (kv,), partner)

        @pl.when(jnp.logical_not(moved))
        def _():
            finr[kv] = total

    def value_wait(d):
        py = ring_y(d + 1)
        arrived(cb.at[1, py], s_va, (py,))

    loop(3, value_wait)
    loop(4, lambda i: grad_tile(1, ring_y(i)))

    arrived(cot.at[1 - xh], s_cot, (0,))

    def wait_partial(kv):
        def body(d):
            py = ring_y(d + 1)
            arrived(precv.at[kv, py], s_p, (kv, py))

        loop(3, body)

    def summed(kv, t, s):
        rows = pl.ds(pl.multiple_of(t * T, T), T)
        cols = slice(s * H, (s + 1) * H)
        total = own[kv, rows, cols]
        for d in range(1, 4):
            total = total + precv[kv, ring_y(d), rows, cols].astype(f32)
        return total

    wait_partial(0)
    hgain = hgain_ref[...]
    vx[x] = jnp.zeros((1, DC + H), f32)

    def key_block(t):
        for s in range(2):
            key = summed(0, t, s)
            krinv = lax.rsqrt(jnp.mean(key * key, axis=-1, keepdims=True) + eps)
            kn = key * krinv
            oown[0, s, t] = (kn * hgain).astype(bf16)
            ct = cot[s, t].astype(f32)
            back = ct * hgain
            grad = krinv * (back - kn * jnp.mean(back * kn, axis=-1, keepdims=True))
            cb[0, y, s, t] = grad.astype(bf16)
            vx[x, :, DC:] += jnp.sum(ct * kn, axis=0, keepdims=True)

    loop(4, key_block)

    def key_gather(i):
        for d in (1, 3, 2):
            py = ring_y(d)
            t = lax.rem(py + 1 + i, 4)
            part = cb.at[0, y, :, t]
            send(part, part, s_ka, (py, t), (y, t), at_y(py))

    loop(4, key_gather)
    send(oown.at[0, 1 - xh], orecv.at[0], s_out, (0,), (0,), opposite)

    loop(4, lambda i: core_sends(1, i))
    loop(4, lambda i: grad_core(1, ring_y(i)))
    grad_tile(0, y)
    loop(4, lambda i: forward(1, i))

    def values_back(i):
        ct = jnp.concatenate(
            [cb[1, i, 0].reshape(4 * T, H), cb[1, i, 1].reshape(4 * T, H)], axis=1
        )
        part = dot_nt(ct, panel(1, i)).reshape(4, T, DC)

        @pl.when(i == 0)
        def _():
            dhv[...] = part

        @pl.when(i > 0)
        def _():
            dhv[...] += part

    loop(4, values_back)

    def hidden_back(i):
        t = ring_y(i + 1)
        for d in range(1, 4):
            py = ring_y(d)
            arrived(cb.at[0, py, :, t], s_ka, (py, t))
        total = dhv[t]
        for k in range(4):
            ct = jnp.concatenate([cb[0, k, 0, t], cb[0, k, 1, t]], axis=1)
            total = total + dot_nt(ct, panel(0, k))
        vx[x, :, :DC] += jnp.sum(total * hc[t].astype(f32), axis=0, keepdims=True)

        @pl.when(t != y)
        def _():
            dhs[t] = total.astype(bf16)
            send(dhs.at[t], dhr.at[y], s_dh, (t,), (y,), at_y(t))

        @pl.when(t == y)
        def _():
            dhr[y] = total.astype(bf16)

    loop(4, hidden_back)
    loop(3, lambda i: grad_tile(0, ring_y(i + 1)))
    for d in (1, 3, 2):
        partial_send(1, d)
    for d in range(1, 4):
        px = ring_x(d)
        send(vx.at[x], vx.at[x], s_vx, (px,), (x,), at_x(px))
    loop(4, lambda i: grad_core(0, ring_y(i)))
    loop(4, lambda i: grad_x(1, ring_y(i)))

    def vec_wait(ref, sems, me, n):
        def body(i):
            p = lax.rem(me + 1 + i, n)
            arrived(ref.at[p], sems, (p,))

        loop(n - 1, body)

    vec_wait(vx, s_vx, x, 4)
    vz[z] = (vx[0] + vx[1]) + (vx[2] + vx[3])

    def vz_send(i):
        pz = ring_z(i + 1)
        send(vz.at[z], vz.at[z], s_vz, (pz,), (z,), at_z(pz))

    loop(7, vz_send)

    def dh_wait(d):
        py = ring_y(d + 1)
        arrived(dhr.at[py], s_dh, (py,))

    loop(3, dh_wait)

    def input_rows(i):
        rows = pl.ds(pl.multiple_of(i * 16, 16), 16)
        rinv = rinv_s[rows, 0:1]
        mean = jnp.zeros((16, 1), f32)
        for k in range(4):
            cols = slice(k * DC, (k + 1) * DC)
            normed = x_ref[rows, cols].astype(f32) * rinv
            back = dhr[k, rows, :].astype(f32) * gain_ref[:, cols]
            mean = mean + jnp.sum(back * normed, axis=-1, keepdims=True)
        mean = mean * (1.0 / D)
        for k in range(4):
            cols = slice(k * DC, (k + 1) * DC)
            normed = x_ref[rows, cols].astype(f32) * rinv
            back = dhr[k, rows, :].astype(f32) * gain_ref[:, cols]
            ig_ref[rows, cols] = (rinv * (back - normed * mean)).astype(bf16)

    loop(8, input_rows)
    vec_wait(vz, s_vz, z, 8)
    vc[c] = ((vz[0] + vz[1]) + (vz[2] + vz[3])) + ((vz[4] + vz[5]) + (vz[6] + vz[7]))
    send(vc.at[c], vc.at[c], s_vc, (0,), (0,), core)
    loop(4, lambda i: grad_x(0, ring_y(i)))

    wait_partial(1)

    def value_block(t):
        for s in range(2):
            oown[1, s, t] = summed(1, t, s).astype(bf16)

    loop(4, value_block)
    send(oown.at[1, 1 - xh], orecv.at[1], s_out, (1,), (1,), opposite)

    arrived(vc.at[1 - c], s_vc, (0,))
    vy[y] = vc[0] + vc[1]
    for d in range(1, 4):
        py = ring_y(d)
        send(vy.at[y], vy.at[y], s_vy, (py,), (y,), at_y(py))

    grad_z(1)
    grad_z(0)

    vec_wait(vy, s_vy, y, 4)
    for k in range(4):
        cols = slice(k * DC, (k + 1) * DC)
        ng_ref[:, cols] = vy[k, :, :DC] / gain_ref[:, cols]
    hg_ref[...] = (vy[0, :, DC:] + vy[1, :, DC:]) + (vy[2, :, DC:] + vy[3, :, DC:])
    for kv, ref in ((0, ks_ref), (1, vs_ref)):
        arrived(orecv.at[kv], s_out, (kv,))
        ref[:, xh] = oown[kv, xh]
        ref[:, 1 - xh] = orecv[kv]
    for kv, ref in ((0, dwk_ref), (1, dwv_ref)):

        @pl.when(moved)
        def _():
            arrived(finr.at[kv], s_dp, (kv,))

        ref[...] = finr[kv]

    @pl.when(moved)
    def _():
        for kv, ref in ((0, wk_ref), (1, wv_ref)):
            sent(ref, s_w0, (kv,))
            sent(fin.at[kv], s_dp, (kv,))

    for kv, ref in ((0, kcot_ref), (1, vcot_ref)):
        sent(ref.at[:, 1 - xh], s_cot, (kv,))
        sent(oown.at[kv, 1 - xh], s_out, (kv,))

    def sent_z(i):
        pz = ring_z(i + 1)
        for kv in range(2):
            sent(w_own(kv), s_wz, (kv, pz))
            sent(zs.at[kv, lax.div(pz, 2), lax.rem(pz, 2)], s_dz, (kv, pz))
        sent(vz.at[z], s_vz, (pz,))

    loop(7, sent_z)

    def sent_x(i):
        px = ring_x(i + 1)
        sent(vx.at[x], s_vx, (px,))
        for kv in range(2):
            for h in range(4):
                sent(w.at[kv, h, xh, :, xl, c], s_wx, (kv, h, px))
                sent(dw.at[kv, h, c, px], s_dx, (kv, h, px))

    loop(3, sent_x)

    def sent_core(h):
        for kv in range(2):
            sent(w.at[kv, h, :, :, :, c], s_wc, (kv, h))
            sent(dw.at[kv, h, 1 - c], s_dc, (kv, h))

    loop(4, sent_core)
    sent(vc.at[c], s_vc, (0,))

    def sent_y(i):
        py = ring_y(i + 1)
        sent(hid.at[py], s_hid, (py,))
        sent(cb.at[1, y], s_va, (py,))
        for t in range(4):
            sent(cb.at[0, y, :, t], s_ka, (py, t))
        for kv in range(2):
            sent(psend.at[kv, py], s_p, (kv, py))
        sent(dhs.at[py], s_dh, (py,))
        sent(vy.at[y], s_vy, (py,))

    loop(3, sent_y)


def on_device(
    inputs, norm_gain, key_weight, value_weight, head_gain, key_cotangent, value_cotangent
):
    def sems(*shape):
        return pltpu.SemaphoreType.DMA((2,) + shape)

    scratch = [
        pltpu.VMEM((4, T, DC), bf16),
        pltpu.VMEM((4, T, DC), bf16),
        pltpu.VMEM((DC, 4 * T), bf16),
        pltpu.VMEM((2, 4, 2, 2, 2, 2, R, H), bf16),
        pltpu.VMEM((2, 4, 4 * T, 2 * H), bf16),
        pltpu.VMEM((2, 4, 4 * T, 2 * H), bf16),
        pltpu.VMEM((2, 4 * T, 2 * H), f32),
        pltpu.VMEM((2, 4, T, H), bf16),
        pltpu.VMEM((2, 4, 2, 4, T, H), bf16),
        pltpu.VMEM((2, 2, 4, T, H), bf16),
        pltpu.VMEM((2, 4, T, H), bf16),
        pltpu.VMEM((4, T, DC), f32),
        pltpu.VMEM((4, T, DC), bf16),
        pltpu.VMEM((4, T, DC), bf16),
        pltpu.VMEM((2, 4, 2, 4, 2, R, H), bf16),
        pltpu.VMEM((2, 4, 4, 2, R, H), bf16),
        pltpu.VMEM((2, 4, 4, 2, R, H), bf16),
        pltpu.VMEM((2, 4, 2, R, H), bf16),
        pltpu.VMEM((2, 8, R, H), bf16),
        pltpu.VMEM((2, R, H), f32),
        pltpu.VMEM((2, R, H), f32),
        pltpu.VMEM((4, 1, DC + H), f32),
        pltpu.VMEM((8, 1, DC + H), f32),
        pltpu.VMEM((2, 1, DC + H), f32),
        pltpu.VMEM((4, 1, DC + H), f32),
        pltpu.VMEM((T, 128), f32),
        sems(2),
        sems(2, 8),
        sems(2, 4, 4),
        sems(2, 4),
        sems(4),
        sems(2),
        sems(4),
        sems(4, 4),
        sems(2, 4),
        sems(2),
        sems(4),
        sems(2, 4),
        sems(2, 4, 4),
        sems(2, 8),
        sems(2),
        sems(4),
        sems(8),
        sems(1),
        sems(4),
    ]
    outs = (
        jax.ShapeDtypeStruct((4, 2, T, H), bf16),
        jax.ShapeDtypeStruct((4, 2, T, H), bf16),
        jax.ShapeDtypeStruct((T, D), bf16),
        jax.ShapeDtypeStruct((R, H), f32),
        jax.ShapeDtypeStruct((R, H), f32),
        jax.ShapeDtypeStruct((1, D), f32),
        jax.ShapeDtypeStruct((1, H), f32),
    )
    vmem = pl.BlockSpec(memory_space=pltpu.VMEM)
    ks, vs, ig, dwk, dwv, ng, hg = pl.pallas_call(
        kernel,
        out_shape=outs,
        in_specs=[vmem] * 7,
        out_specs=(vmem,) * 7,
        scratch_shapes=scratch,
        compiler_params=pltpu.CompilerParams(
            collective_id=0, has_side_effects=True, vmem_limit_bytes=60 * 1024 * 1024
        ),
        cost_estimate=pl.CostEstimate(
            flops=6 * 512 * DC * 2048, bytes_accessed=6 * 1024 * 1024, transcendentals=0
        ),
    )(
        inputs,
        norm_gain.astype(f32).reshape(1, D),
        key_weight,
        value_weight,
        head_gain.astype(f32).reshape(1, H),
        key_cotangent.reshape(4, 2, T, H),
        value_cotangent.reshape(4, 2, T, H),
    )
    return (
        ks.reshape(8 * T, H),
        vs.reshape(8 * T, H),
        ig,
        dwk,
        dwv,
        ng.reshape(D),
        hg.reshape(H),
    )


def solution(mesh):
    in_specs = (
        P(("dp", "tensor"), None),
        P(),
        P("dp", "tensor"),
        P("dp", "tensor"),
        P(),
        P("dp", "tensor"),
        P("dp", "tensor"),
    )
    out_specs = (
        P("dp", "tensor"),
        P("dp", "tensor"),
        P(("dp", "tensor"), None),
        P("dp", "tensor"),
        P("dp", "tensor"),
        P(),
        P(),
    )
    return jax.shard_map(
        on_device, mesh=mesh, in_specs=in_specs, out_specs=out_specs, check_vma=False
    )
```

time: 725 us -> 123 us (0.17)
  the two profiles are of different devices: /device:TPU:16 before, /device:TPU:242 now
where the time goes in v1:
time: 123 us
  Pallas kernels  111 us (90%)
  local copies, waits for them, and re-layouts  8.24 us (7%)
  other arithmetic  2.48 us (2%)
    pallas_call x1, Pallas kernels, on_device(): pl.pallas_call(kernel, out_shape=outs, in_specs=[vmem] * 7, out_specs=(vm...  111 us
    unnamed x15, local copies, waits for them, and re-layouts  8.24 us

profile of v1, /device:TPU:242, one launch (start us, length us, event | category | flops | bytes accessed | tf_op | source)
XLA Modules:
  0.0 122.6 jit_solution(16442117877769521692)
XLA Ops:
  0.6 1.2 bitcast_convert_fusion.hgain_ref
  1.8 1.3 %reshape.52 = f32[5120]{0:T(1024)} convert(bf16[5120]{0:T(1024)(128)(2,1)} %param.8) | non-fusion elementwise | flops 5120 | bytes 30720 | tf_op jit(solution)/shard_map/reshape | solution.py:665
  3.1 111.3 %shard_map.126 = (bf16[4,2,128,128]{3,2,1,0:T(8,128)(2,1)}, bf16[4,2,128,128]{3,2,1,0:T(8,128)(2,1)}, bf16[128,5120]{1,0:T(8,128)(2,1)}, f32[160,128]{1,0:T(8,12...) custom-call(bf16[128,5120]{1,0:T(8,128)(2,1)} %x_ref.1, f32[1,5120]{1,0:T(1,128)} %bitcast.13, ...), custom_call_target="tpu_custom_call" | custom-call | flops 8053063680 | bytes 6291456 | tf_op jit(solution)/shard_map/pallas_call | solution.py:651
  114.4 1.7 %copy.21 = bf16[1024,128]{1,0:T(8,128)(2,1)} copy(bf16[1024,128]{1,0:T(8,128)(2,1)} %bitcast.11) | data formatting | bytes 524288
  116.0 1.7 %copy.22 = bf16[1024,128]{1,0:T(8,128)(2,1)} copy(bf16[1024,128]{1,0:T(8,128)(2,1)} %bitcast.10) | data formatting | bytes 524288
  117.7 0.0 copy-start.1
  117.7 0.0 copy-start
  117.7 0.0 copy-start.2
  117.7 0.0 copy-start.3
  117.7 2.5 %copy.23 = bf16[128,5120]{1,0:T(8,128)(2,1)} copy(bf16[128,5120]{1,0:T(8,128)(2,1)} %get-tuple-element.30) | data formatting | bytes 2621440
  120.2 0.0 copy-done.1
  120.2 0.6 copy.24
  120.9 0.0 copy-done
  120.9 0.6 copy.25
  121.5 0.0 copy-done.2
  121.5 0.6 copy.26
  122.1 0.0 copy-done.3
  122.1 0.5 copy.27
Async XLA Ops:
  117.7 2.5 %copy-start.1 = (f32[160,128]{1,0:T(8,128)S(1)}, f32[160,128]{1,0:T(8,128)}, u32[]{:S(2)}) copy-start(f32[160,128]{1,0:T(8,128)} %get-tuple-element.31) | copy-start | bytes 245764
  117.7 3.1 %copy-start = (f32[160,128]{1,0:T(8,128)S(1)}, f32[160,128]{1,0:T(8,128)}, u32[]{:S(2)}) copy-start(f32[160,128]{1,0:T(8,128)} %get-tuple-element.32) | copy-start | bytes 245764
  117.7 3.8 %copy-start.2 = (f32[1,5120]{1,0:T(1,128)S(1)}, f32[1,5120]{1,0:T(1,128)}, u32[]{:S(2)}) copy-start(f32[1,5120]{1,0:T(1,128)} %get-tuple-element.19) | copy-start | bytes 61444
  117.7 4.4 %copy-start.3 = (f32[1,128]{1,0:T(1,128)S(1)}, f32[1,128]{1,0:T(1,128)}, u32[]{:S(2)}) copy-start(f32[1,128]{1,0:T(1,128)} %get-tuple-element.20) | copy-start | bytes 1540

commit v2 on v1

--- a/solution.py
+++ b/solution.py
@@ -11,6 +11,7 @@
 D = 5120
 DC = 1280
 R = 160
+RA = 128
 H = 128
 bf16 = jnp.bfloat16
 f32 = jnp.float32
@@ -33,7 +34,7 @@
 
 
 def kernel(
-    x_ref,
+    x_hbm,
     gain_ref,
     wk_ref,
     wv_ref,
@@ -73,14 +74,17 @@
     vc,
     vy,
     rinv_s,
+    gain_s,
+    x_ref,
     s_w0,
     s_wz,
     s_wx,
+    s_wy,
+    s_wr,
     s_wc,
     s_hid,
     s_cot,
-    s_va,
-    s_ka,
+    s_ag,
     s_p,
     s_out,
     s_dh,
@@ -92,6 +96,7 @@
     s_vz,
     s_vc,
     s_vy,
+    s_in,
 ):
     dp, tn = lax.axis_index("dp"), lax.axis_index("tensor")
     z, xl, c = lax.div(dp, 4), lax.rem(lax.div(dp, 2), 2), lax.rem(dp, 2)
@@ -167,53 +172,87 @@
     def _():
         hello(partner)
 
+    local = [
+        pltpu.make_async_copy(x_hbm, x_ref, s_in.at[0]),
+        pltpu.make_async_copy(vcot_ref.at[:, xh], cb.at[1, y, xh], s_in.at[1]),
+        pltpu.make_async_copy(kcot_ref.at[:, xh], cot.at[xh], s_in.at[2]),
+    ]
+    for copy in local:
+        copy.start()
+    for k in range(D // 128):
+        gain_s[:, k * 128 : (k + 1) * 128] = gain_ref[k : k + 1, :].astype(f32)
+
+    def w_own(kv):
+        return w.at[kv, zh, xh, ze, xl, c]
+
+    @pl.when(jnp.logical_not(moved))
+    def _():
+        for kv, ref in ((0, wk_ref), (1, wv_ref)):
+            w[kv, zh, xh, ze, xl, c] = ref[...]
+
+    pl.semaphore_wait(barrier, jnp.where(moved, 15, 14))
+
+    def w_move(kv):
+        @pl.when(moved)
+        def _():
+            ref = (wk_ref, wv_ref)[kv]
+            send(ref, w.at[kv, y, xh, ze, xl, c], s_w0, (kv,), (kv,), partner)
+
+    w_move(0)
+    send(vcot_ref.at[:, 1 - xh], cb.at[1, y, xh], s_cot, (1,), (1,), opposite)
+
     def norm_rows(i):
         rows = pl.ds(pl.multiple_of(i * 16, 16), 16)
         xf = x_ref[rows, :].astype(f32)
         rinv = lax.rsqrt(jnp.mean(xf * xf, axis=-1, keepdims=True) + eps)
         rinv_s[rows, :] = jnp.broadcast_to(rinv, (16, 128))
-        hd = (xf * rinv * gain_ref[...]).astype(bf16)
+        hd = (xf * rinv * gain_s[...]).astype(bf16)
         for k in range(4):
             hid[k, rows, :] = hd[:, k * DC : (k + 1) * DC]
 
+    local[0].wait()
     loop(8, norm_rows)
-    hc[y] = hid[y]
-    cb[1, y, xh] = vcot_ref[:, xh]
-    cot[xh] = kcot_ref[:, xh]
-
-    pl.semaphore_wait(barrier, jnp.where(moved, 15, 14))
-
-    def w_own(kv):
-        return w.at[kv, zh, xh, ze, xl, c]
-
-    @pl.when(moved)
-    def _():
-        for kv, ref in ((0, wk_ref), (1, wv_ref)):
-            send(ref, w.at[kv, y, xh, ze, xl, c], s_w0, (kv,), (kv,), partner)
-
-    @pl.when(jnp.logical_not(moved))
-    def _():
-        for kv, ref in ((0, wk_ref), (1, wv_ref)):
-            w[kv, zh, xh, ze, xl, c] = ref[...]
-
     for d in (1, 3, 2):
         py = ring_y(d)
         send(hid.at[py], hc.at[y], s_hid, (py,), (y,), at_y(py))
-    send(vcot_ref.at[:, 1 - xh], cb.at[1, y, xh], s_cot, (1,), (1,), opposite)
-    send(kcot_ref.at[:, 1 - xh], cot.at[xh], s_cot, (0,), (0,), opposite)
-
-    def z_sends(kv):
+    hc[y] = hid[y]
+    local[1].wait()
+    local[2].wait()
+
+
+    def moved_in(kv):
         @pl.when(moved)
         def _():
             arrived(w_own(kv), s_w0, (kv,))
 
-        def body(i):
+    def w_first(kv):
+        moved_in(kv)
+        part = w.at[kv, zh, xh, ze, xl, c, 0:RA]
+
+        def z_send(i):
             pz = ring_z(i + 1)
-            send(w_own(kv), w_own(kv), s_wz, (kv, pz), (kv, z), at_z(pz))
-
-        loop(7, body)
-
-    def x_sends(kv, i):
+            send(part, part, s_wz, (kv, pz), (kv, z), at_z(pz))
+
+        loop(7, z_send)
+        rest = w.at[kv, zh, xh, ze, xl, c, RA:R]
+        for d in (1, 3, 2):
+            px = ring_x(d)
+            send(rest, rest, s_wy, (kv, px), (kv, x), at_x(px))
+
+    def w_second(kv):
+        for d in range(1, 4):
+            px = ring_x(d)
+            pxl, pxh = lax.rem(px, 2), lax.div(px, 2)
+            arrived(w.at[kv, zh, pxh, ze, pxl, c, RA:R], s_wy, (kv, px))
+        part = w.at[kv, zh, :, ze, :, c, RA:R]
+
+        def z_send(i):
+            pz = ring_z(i + 1)
+            send(part, part, s_wr, (kv, pz), (kv, z), at_z(pz))
+
+        loop(7, z_send)
+
+    def w_x(kv, i):
         h = ring_y(i + 1)
 
         def wait_z(e):
@@ -221,46 +260,49 @@
 
             @pl.when(pz != z)
             def _():
-                arrived(w.at[kv, h, xh, e, xl, c], s_wz, (kv, pz))
+                arrived(w.at[kv, h, xh, e, xl, c, 0:RA], s_wz, (kv, pz))
 
         loop(2, wait_z)
-        part = w.at[kv, h, xh, :, xl, c]
+        part = w.at[kv, h, xh, :, xl, c, 0:RA]
         for d in (1, 3, 2):
             px = ring_x(d)
             send(part, part, s_wx, (kv, h, px), (kv, h, x), at_x(px))
 
-    def core_sends(kv, i):
+    def w_core(kv, i):
         h = ring_y(i + 1)
 
         def wait_x(d):
             px = ring_x(d + 1)
             pxl, pxh = lax.rem(px, 2), lax.div(px, 2)
-            arrived(w.at[kv, h, pxh, :, pxl, c], s_wx, (kv, h, px))
+            arrived(w.at[kv, h, pxh, :, pxl, c, 0:RA], s_wx, (kv, h, px))
+
+        def wait_z(e):
+            pz = 2 * h + e
+
+            @pl.when(pz != z)
+            def _():
+                arrived(w.at[kv, h, :, e, :, c, RA:R], s_wr, (kv, pz))
 
         loop(3, wait_x)
+        loop(2, wait_z)
         part = w.at[kv, h, :, :, :, c]
         send(part, part, s_wc, (kv, h), (kv, h), core)
 
-    z_sends(0)
-    z_sends(1)
-    arrived(cb.at[1, y, 1 - xh], s_cot, (1,))
-    for d in (1, 3, 2):
-        py = ring_y(d)
-        send(cb.at[1, y], cb.at[1, y], s_va, (py,), (y,), at_y(py))
-    loop(4, lambda i: x_sends(0, i))
+    w_first(0)
+    w_move(1)
+    loop(4, lambda i: w_x(0, i))
+    w_second(0)
+    w_first(1)
+    send(kcot_ref.at[:, 1 - xh], cot.at[xh], s_cot, (0,), (0,), opposite)
 
     def panel(kv, h):
         return jnp.concatenate(
             [w[kv, h, 0].reshape(DC, H), w[kv, h, 1].reshape(DC, H)], axis=1
         )
 
-    def tokens():
-        return hc[...].reshape(4 * T, DC)
-
     def forward(kv, i):
         h = ring_y(i + 1)
-        arrived(w.at[kv, h, :, :, :, 1 - c], s_wc, (kv, h))
-        part = dot(tokens(), panel(kv, h))
+        part = dot(hc[...].reshape(4 * T, DC), panel(kv, h))
 
         @pl.when(h != y)
         def _():
@@ -280,30 +322,56 @@
 
     loop(3, hidden_wait)
 
-    def key_step(i):
-        @pl.when(i < 4)
-        def _():
-            core_sends(0, i)
-            x_sends(1, i)
-
-        @pl.when(i > 0)
-        def _():
-            forward(0, i - 1)
-
-        @pl.when(jnp.logical_and(i > 0, i < 4))
-        def _():
-            partial_send(0, i)
-
-    loop(5, key_step)
-
+    def gather(kv):
+        for d, slot in ((1, 0), (3, 1)):
+            send(cb.at[kv, y], cb.at[kv, y], s_ag, (kv, slot), (kv, slot), at_y(ring_y(d)))
+
+    def gather_near(kv):
+        for d, slot in ((3, 0), (1, 1)):
+            arrived(cb.at[kv, ring_y(d)], s_ag, (kv, slot))
+        for d, to, half, slot in ((3, 1, 0, 2), (1, 3, 2, 3)):
+            part = cb.at[kv, ring_y(d), :, half : half + 2]
+            send(part, part, s_ag, (kv, slot), (kv, slot), at_y(ring_y(to)))
+
+    def gather_far(kv):
+        for half, slot in ((0, 2), (2, 3)):
+            arrived(cb.at[kv, ring_y(2), :, half : half + 2], s_ag, (kv, slot))
+
+    arrived(cb.at[1, y, 1 - xh], s_cot, (1,))
+    gather(1)
     for k in range(4):
         hct[:, k * T : (k + 1) * T] = hc[k].T
 
-    def grad_tile(kv, h):
-        ct = jnp.concatenate(
+    def key_tile(i):
+        h = ring_y(i + 1)
+        arrived(w.at[0, h, :, :, :, 1 - c], s_wc, (0, h))
+        forward(0, i)
+
+        @pl.when(i < 3)
+        def _():
+            partial_send(0, i + 1)
+
+    def key_step(i):
+        w_core(0, i)
+
+        @pl.when(i > 0)
+        def _():
+            key_tile(i - 1)
+
+    loop(3, key_step)
+    w_second(1)
+    loop(4, lambda i: w_x(1, i))
+    key_step(3)
+    key_tile(3)
+    gather_near(1)
+
+    def cots(kv, h):
+        return jnp.concatenate(
             [cb[kv, h, 0].reshape(4 * T, H), cb[kv, h, 1].reshape(4 * T, H)], axis=1
         )
-        g = dot(hct[...], ct).astype(bf16).reshape(2, 2, 2, R, 2 * H)
+
+    def grad_tile(kv, h):
+        g = dot(hct[...], cots(kv, h)).astype(bf16).reshape(2, 2, 2, R, 2 * H)
         for pc in range(2):
             for ph in range(2):
                 for pxl in range(2):
@@ -352,12 +420,8 @@
         def _():
             finr[kv] = total
 
-    def value_wait(d):
-        py = ring_y(d + 1)
-        arrived(cb.at[1, py], s_va, (py,))
-
-    loop(3, value_wait)
-    loop(4, lambda i: grad_tile(1, ring_y(i)))
+    loop(3, lambda i: grad_tile(1, ring_y(i + lax.div(i, 2))))
+    loop(3, lambda i: grad_core(1, ring_y(i + lax.div(i, 2))))
 
     arrived(cot.at[1 - xh], s_cot, (0,))
 
@@ -377,7 +441,7 @@
         return total
 
     wait_partial(0)
-    hgain = hgain_ref[...]
+    hgain = hgain_ref[...].astype(f32)
     vx[x] = jnp.zeros((1, DC + H), f32)
 
     def key_block(t):
@@ -393,47 +457,46 @@
             vx[x, :, DC:] += jnp.sum(ct * kn, axis=0, keepdims=True)
 
     loop(4, key_block)
-
-    def key_gather(i):
-        for d in (1, 3, 2):
-            py = ring_y(d)
-            t = lax.rem(py + 1 + i, 4)
-            part = cb.at[0, y, :, t]
-            send(part, part, s_ka, (py, t), (y, t), at_y(py))
-
-    loop(4, key_gather)
+    gather(0)
     send(oown.at[0, 1 - xh], orecv.at[0], s_out, (0,), (0,), opposite)
 
-    loop(4, lambda i: core_sends(1, i))
-    loop(4, lambda i: grad_core(1, ring_y(i)))
+    def back_panel(kv, h, first):
+        part = dot_nt(cots(kv, h), panel(kv, h)).reshape(4, T, DC)
+        if first:
+            dhv[...] = part
+        else:
+            dhv[...] += part
+
+    gather_far(1)
+    grad_tile(1, ring_y(2))
     grad_tile(0, y)
-    loop(4, lambda i: forward(1, i))
-
-    def values_back(i):
-        ct = jnp.concatenate(
-            [cb[1, i, 0].reshape(4 * T, H), cb[1, i, 1].reshape(4 * T, H)], axis=1
-        )
-        part = dot_nt(ct, panel(1, i)).reshape(4, T, DC)
-
-        @pl.when(i == 0)
-        def _():
-            dhv[...] = part
-
-        @pl.when(i > 0)
-        def _():
-            dhv[...] += part
-
-    loop(4, values_back)
+    back_panel(0, y, True)
+    grad_core(1, ring_y(2))
+    grad_core(0, y)
+    loop(4, lambda i: w_core(1, i))
+    gather_near(0)
+
+    def value_tile(i):
+        h = ring_y(i + 1)
+        arrived(w.at[1, h, :, :, :, 1 - c], s_wc, (1, h))
+        forward(1, i)
+
+        @pl.when(i < 3)
+        def _():
+            partial_send(1, i + 1)
+
+    loop(4, value_tile)
+    loop(2, lambda i: grad_tile(0, ring_y(2 * i + 1)))
+    loop(4, lambda i: back_panel(1, i, False))
+    loop(2, lambda i: grad_core(0, ring_y(2 * i + 1)))
+    loop(2, lambda i: back_panel(0, ring_y(2 * i + 1), False))
+    gather_far(0)
 
     def hidden_back(i):
         t = ring_y(i + 1)
-        for d in range(1, 4):
-            py = ring_y(d)
-            arrived(cb.at[0, py, :, t], s_ka, (py, t))
-        total = dhv[t]
-        for k in range(4):
-            ct = jnp.concatenate([cb[0, k, 0, t], cb[0, k, 1, t]], axis=1)
-            total = total + dot_nt(ct, panel(0, k))
+        far = ring_y(2)
+        ct = jnp.concatenate([cb[0, far, 0, t], cb[0, far, 1, t]], axis=1)
+        total = dhv[t] + dot_nt(ct, panel(0, far))
         vx[x, :, :DC] += jnp.sum(total * hc[t].astype(f32), axis=0, keepdims=True)
 
         @pl.when(t != y)
@@ -446,14 +509,12 @@
             dhr[y] = total.astype(bf16)
 
     loop(4, hidden_back)
-    loop(3, lambda i: grad_tile(0, ring_y(i + 1)))
-    for d in (1, 3, 2):
-        partial_send(1, d)
     for d in range(1, 4):
         px = ring_x(d)
         send(vx.at[x], vx.at[x], s_vx, (px,), (x,), at_x(px))
-    loop(4, lambda i: grad_core(0, ring_y(i)))
-    loop(4, lambda i: grad_x(1, ring_y(i)))
+    grad_tile(0, ring_y(2))
+
+    grad_core(0, ring_y(2))
 
     def vec_wait(ref, sems, me, n):
         def body(i):
@@ -462,6 +523,7 @@
 
         loop(n - 1, body)
 
+    loop(4, lambda i: grad_x(1, ring_y(i)))
     vec_wait(vx, s_vx, x, 4)
     vz[z] = (vx[0] + vx[1]) + (vx[2] + vx[3])
 
@@ -470,6 +532,27 @@
         send(vz.at[z], vz.at[z], s_vz, (pz,), (z,), at_z(pz))
 
     loop(7, vz_send)
+    grad_x(0, y)
+    loop(2, lambda i: grad_x(0, ring_y(2 * i + 1)))
+    grad_z(1)
+    vec_wait(vz, s_vz, z, 8)
+    vc[c] = ((vz[0] + vz[1]) + (vz[2] + vz[3])) + ((vz[4] + vz[5]) + (vz[6] + vz[7]))
+    send(vc.at[c], vc.at[c], s_vc, (0,), (0,), core)
+    grad_x(0, ring_y(2))
+    arrived(vc.at[1 - c], s_vc, (0,))
+    vy[y] = vc[0] + vc[1]
+    for d in range(1, 4):
+        py = ring_y(d)
+        send(vy.at[y], vy.at[y], s_vy, (py,), (y,), at_y(py))
+
+    wait_partial(1)
+
+    def value_block(t):
+        for s in range(2):
+            oown[1, s, t] = summed(1, t, s).astype(bf16)
+
+    loop(4, value_block)
+    send(oown.at[1, 1 - xh], orecv.at[1], s_out, (1,), (1,), opposite)
 
     def dh_wait(d):
         py = ring_y(d + 1)
@@ -484,43 +567,22 @@
         for k in range(4):
             cols = slice(k * DC, (k + 1) * DC)
             normed = x_ref[rows, cols].astype(f32) * rinv
-            back = dhr[k, rows, :].astype(f32) * gain_ref[:, cols]
+            back = dhr[k, rows, :].astype(f32) * gain_s[:, cols]
             mean = mean + jnp.sum(back * normed, axis=-1, keepdims=True)
         mean = mean * (1.0 / D)
         for k in range(4):
             cols = slice(k * DC, (k + 1) * DC)
             normed = x_ref[rows, cols].astype(f32) * rinv
-            back = dhr[k, rows, :].astype(f32) * gain_ref[:, cols]
+            back = dhr[k, rows, :].astype(f32) * gain_s[:, cols]
             ig_ref[rows, cols] = (rinv * (back - normed * mean)).astype(bf16)
 
     loop(8, input_rows)
-    vec_wait(vz, s_vz, z, 8)
-    vc[c] = ((vz[0] + vz[1]) + (vz[2] + vz[3])) + ((vz[4] + vz[5]) + (vz[6] + vz[7]))
-    send(vc.at[c], vc.at[c], s_vc, (0,), (0,), core)
-    loop(4, lambda i: grad_x(0, ring_y(i)))
-
-    wait_partial(1)
-
-    def value_block(t):
-        for s in range(2):
-            oown[1, s, t] = summed(1, t, s).astype(bf16)
-
-    loop(4, value_block)
-    send(oown.at[1, 1 - xh], orecv.at[1], s_out, (1,), (1,), opposite)
-
-    arrived(vc.at[1 - c], s_vc, (0,))
-    vy[y] = vc[0] + vc[1]
-    for d in range(1, 4):
-        py = ring_y(d)
-        send(vy.at[y], vy.at[y], s_vy, (py,), (y,), at_y(py))
-
-    grad_z(1)
     grad_z(0)
 
     vec_wait(vy, s_vy, y, 4)
     for k in range(4):
         cols = slice(k * DC, (k + 1) * DC)
-        ng_ref[:, cols] = vy[k, :, :DC] / gain_ref[:, cols]
+        ng_ref[:, cols] = vy[k, :, :DC] / gain_s[:, cols]
     hg_ref[...] = (vy[0, :, DC:] + vy[1, :, DC:]) + (vy[2, :, DC:] + vy[3, :, DC:])
     for kv, ref in ((0, ks_ref), (1, vs_ref)):
         arrived(orecv.at[kv], s_out, (kv,))
@@ -547,7 +609,8 @@
     def sent_z(i):
         pz = ring_z(i + 1)
         for kv in range(2):
-            sent(w_own(kv), s_wz, (kv, pz))
+            sent(w.at[kv, zh, xh, ze, xl, c, 0:RA], s_wz, (kv, pz))
+            sent(w.at[kv, zh, :, ze, :, c, RA:R], s_wr, (kv, pz))
             sent(zs.at[kv, lax.div(pz, 2), lax.rem(pz, 2)], s_dz, (kv, pz))
         sent(vz.at[z], s_vz, (pz,))
 
@@ -557,8 +620,9 @@
         px = ring_x(i + 1)
         sent(vx.at[x], s_vx, (px,))
         for kv in range(2):
+            sent(w.at[kv, zh, xh, ze, xl, c, RA:R], s_wy, (kv, px))
             for h in range(4):
-                sent(w.at[kv, h, xh, :, xl, c], s_wx, (kv, h, px))
+                sent(w.at[kv, h, xh, :, xl, c, 0:RA], s_wx, (kv, h, px))
                 sent(dw.at[kv, h, c, px], s_dx, (kv, h, px))
 
     loop(3, sent_x)
@@ -570,19 +634,33 @@
 
     loop(4, sent_core)
     sent(vc.at[c], s_vc, (0,))
+    for kv in range(2):
+        for slot in range(2):
+            sent(cb.at[kv, y], s_ag, (kv, slot))
+            sent(cb.at[kv, y, :, 0:2], s_ag, (kv, slot + 2))
 
     def sent_y(i):
         py = ring_y(i + 1)
         sent(hid.at[py], s_hid, (py,))
-        sent(cb.at[1, y], s_va, (py,))
-        for t in range(4):
-            sent(cb.at[0, y, :, t], s_ka, (py, t))
         for kv in range(2):
             sent(psend.at[kv, py], s_p, (kv, py))
         sent(dhs.at[py], s_dh, (py,))
         sent(vy.at[y], s_vy, (py,))
 
     loop(3, sent_y)
+
+
+def hand_out(*refs):
+    ins, outs, held, sems = refs[:7], refs[7:14], refs[14:21], refs[21]
+    first = [pltpu.make_async_copy(ins[i], held[i], sems.at[0, i]) for i in range(7)]
+    last = [pltpu.make_async_copy(held[i], outs[i], sems.at[1, i]) for i in range(7)]
+    for copy in first:
+        copy.start()
+    for i in range(7):
+        first[i].wait()
+        last[i].start()
+    for copy in last:
+        copy.wait()
 
 
 def on_device(
@@ -618,14 +696,17 @@
         pltpu.VMEM((2, 1, DC + H), f32),
         pltpu.VMEM((4, 1, DC + H), f32),
         pltpu.VMEM((T, 128), f32),
+        pltpu.VMEM((1, D), f32),
+        pltpu.VMEM((T, D), bf16),
         sems(2),
         sems(2, 8),
         sems(2, 4, 4),
         sems(2, 4),
+        sems(2, 8),
+        sems(2, 4),
         sems(4),
         sems(2),
-        sems(4),
-        sems(4, 4),
+        sems(2, 4),
         sems(2, 4),
         sems(2),
         sems(4),
@@ -637,6 +718,7 @@
         sems(8),
         sems(1),
         sems(4),
+        pltpu.SemaphoreType.DMA((3,)),
     ]
     outs = (
         jax.ShapeDtypeStruct((4, 2, T, H), bf16),
@@ -648,10 +730,11 @@
         jax.ShapeDtypeStruct((1, H), f32),
     )
     vmem = pl.BlockSpec(memory_space=pltpu.VMEM)
-    ks, vs, ig, dwk, dwv, ng, hg = pl.pallas_call(
+    anywhere = pl.BlockSpec(memory_space=pl.ANY)
+    results = pl.pallas_call(
         kernel,
         out_shape=outs,
-        in_specs=[vmem] * 7,
+        in_specs=[anywhere, vmem, vmem, vmem, vmem, anywhere, anywhere],
         out_specs=(vmem,) * 7,
         scratch_shapes=scratch,
         compiler_params=pltpu.CompilerParams(
@@ -662,13 +745,22 @@
         ),
     )(
         inputs,
-        norm_gain.astype(f32).reshape(1, D),
+        norm_gain.reshape(D // 128, 128),
         key_weight,
         value_weight,
-        head_gain.astype(f32).reshape(1, H),
+        head_gain.reshape(1, H),
         key_cotangent.reshape(4, 2, T, H),
         value_cotangent.reshape(4, 2, T, H),
     )
+    ks, vs, ig, dwk, dwv, ng, hg = pl.pallas_call(
+        hand_out,
+        out_shape=outs,
+        in_specs=[pl.BlockSpec(memory_space=pl.ANY)] * 7,
+        out_specs=(pl.BlockSpec(memory_space=pl.ANY),) * 7,
+        scratch_shapes=[pltpu.VMEM(o.shape, o.dtype) for o in outs]
+        + [pltpu.SemaphoreType.DMA((2, 7))],
+        compiler_params=pltpu.CompilerParams(vmem_limit_bytes=60 * 1024 * 1024),
+    )(*results)
     return (
         ks.reshape(8 * T, H),
         vs.reshape(8 * T, H),

time: 123 us -> 107 us (0.87)
  the two profiles are of different devices: /device:TPU:242 before, /device:TPU:16 now
where the time goes in v2:
time: 107 us
  Pallas kernels  106 us (99%)
    pallas_call x1, Pallas kernels, on_device(): pl.pallas_call(kernel, out_shape=outs, in_specs=[anywhere, vmem, vmem, vm...  104 us
    pallas_call x1, Pallas kernels, on_device(): pl.pallas_call(hand_out, out_shape=outs, in_specs=[pl.BlockSpec(memory_sp...  2.71 us

profile of v2, /device:TPU:16, one launch (start us, length us, event | category | flops | bytes accessed | tf_op | source)
XLA Modules:
  0.0 106.9 jit_solution(642033179730880694)
XLA Ops:
  0.6 103.5 %shard_map.126 = (bf16[4,2,128,128]{3,2,1,0:T(8,128)(2,1)}, bf16[4,2,128,128]{3,2,1,0:T(8,128)(2,1)}, bf16[128,5120]{1,0:T(8,128)(2,1)}, f32[160,128]{1,0:T(8,12...) custom-call(bf16[128,5120]{1,0:T(8,128)(2,1)} %x_hbm.1, bf16[40,128]{1,0:T(8,128)(2,1)} %bitcast.13, ...), custom_call_target="tpu_custom_call" | custom-call | flops 8053063680 | bytes 6291456 | tf_op jit(solution)/shard_map/pallas_call | solution.py:734
  104.2 2.7 %shard_map.127 = (bf16[4,2,128,128]{3,2,1,0:T(8,128)(2,1)}, bf16[4,2,128,128]{3,2,1,0:T(8,128)(2,1)}, bf16[128,5120]{1,0:T(8,128)(2,1)}, f32[160,128]{1,0:T(8,12...) custom-call(bf16[4,2,128,128]{3,2,1,0:T(8,128)(2,1)} %get-tuple-element.21.refs_0_, ...), custom_call_target="tpu_custom_call" | custom-call | tf_op jit(solution)/shard_map/pallas_call | solution.py:755

commit v3 on v2

--- a/solution.py
+++ b/solution.py
@@ -11,7 +11,7 @@
 D = 5120
 DC = 1280
 R = 160
-RA = 128
+RA = 112
 H = 128
 bf16 = jnp.bfloat16
 f32 = jnp.float32
@@ -54,6 +54,7 @@
     w,
     psend,
     precv,
+    pfar,
     own,
     cot,
     cb,
@@ -65,6 +66,8 @@
     dw,
     dwc,
     dwx,
+    dwf,
+    dwd,
     zs,
     zr,
     fin,
@@ -86,10 +89,13 @@
     s_cot,
     s_ag,
     s_p,
+    s_pf,
+    s_pn,
     s_out,
     s_dh,
     s_dc,
     s_dx,
+    s_df,
     s_dz,
     s_dp,
     s_vx,
@@ -264,17 +270,27 @@
 
         loop(2, wait_z)
         part = w.at[kv, h, xh, :, xl, c, 0:RA]
-        for d in (1, 3, 2):
-            px = ring_x(d)
-            send(part, part, s_wx, (kv, h, px), (kv, h, x), at_x(px))
+        for d, slot in ((1, 0), (3, 1)):
+            send(part, part, s_wx, (kv, h, slot), (kv, h, slot), at_x(ring_x(d)))
+
+    def of_x(kv, h, px):
+        return w.at[kv, h, lax.div(px, 2), :, lax.rem(px, 2), c, 0:RA]
+
+    def far_x(kv, h, px, e):
+        return w.at[kv, h, lax.div(px, 2), e, lax.rem(px, 2), c, 0:RA]
+
+    def w_on(kv, i):
+        h = ring_y(i + 1)
+        for d, slot in ((3, 0), (1, 1)):
+            arrived(of_x(kv, h, ring_x(d)), s_wx, (kv, h, slot))
+        for d, to, e in ((3, 1, 0), (1, 3, 1)):
+            part = far_x(kv, h, ring_x(d), e)
+            send(part, part, s_wx, (kv, h, 2 + e), (kv, h, 2 + e), at_x(ring_x(to)))
 
     def w_core(kv, i):
         h = ring_y(i + 1)
-
-        def wait_x(d):
-            px = ring_x(d + 1)
-            pxl, pxh = lax.rem(px, 2), lax.div(px, 2)
-            arrived(w.at[kv, h, pxh, :, pxl, c, 0:RA], s_wx, (kv, h, px))
+        for e in range(2):
+            arrived(far_x(kv, h, ring_x(2), e), s_wx, (kv, h, 2 + e))
 
         def wait_z(e):
             pz = 2 * h + e
@@ -283,7 +299,6 @@
             def _():
                 arrived(w.at[kv, h, :, e, :, c, RA:R], s_wr, (kv, pz))
 
-        loop(3, wait_x)
         loop(2, wait_z)
         part = w.at[kv, h, :, :, :, c]
         send(part, part, s_wc, (kv, h), (kv, h), core)
@@ -293,6 +308,7 @@
     loop(4, lambda i: w_x(0, i))
     w_second(0)
     w_first(1)
+    loop(4, lambda i: w_on(0, i))
     send(kcot_ref.at[:, 1 - xh], cot.at[xh], s_cot, (0,), (0,), opposite)
 
     def panel(kv, h):
@@ -315,6 +331,27 @@
     def partial_send(kv, d):
         py = ring_y(d)
         send(psend.at[kv, py], precv.at[kv, y], s_p, (kv, py), (kv, y), at_y(py))
+
+    def halves(ref, half):
+        return ref.at[half * 2 * T : (half + 1) * 2 * T]
+
+    def far_send():
+        for d, half in ((1, 0), (3, 1)):
+            part = halves(psend.at[1, ring_y(2)], half)
+            send(part, pfar.at[half], s_pf, (half,), (half,), at_y(ring_y(d)))
+
+    def near_send(d, slot, half):
+        src = halves(psend.at[1, ring_y(d)], half)
+        dst = halves(precv.at[1, slot], half)
+        send(src, dst, s_pn, (slot, half), (slot, half), at_y(ring_y(d)))
+
+    def near_added():
+        for d, slot in ((1, 0), (3, 1)):
+            arrived(pfar.at[slot], s_pf, (slot,))
+            rows = slice(slot * 2 * T, (slot + 1) * 2 * T)
+            total = psend[1, ring_y(d), rows].astype(f32) + pfar[slot].astype(f32)
+            psend[1, ring_y(d), rows] = total.astype(bf16)
+            near_send(d, slot, slot)
 
     def hidden_wait(d):
         py = ring_y(d + 1)
@@ -358,12 +395,11 @@
         def _():
             key_tile(i - 1)
 
-    loop(3, key_step)
+    loop(4, key_step)
+    key_tile(3)
+    gather_near(1)
     w_second(1)
     loop(4, lambda i: w_x(1, i))
-    key_step(3)
-    key_tile(3)
-    gather_near(1)
 
     def cots(kv, h):
         return jnp.concatenate(
@@ -378,21 +414,45 @@
                     dw[kv, h, pc, 2 * ph + pxl] = g[:, pxl, pc, :, ph * H : (ph + 1) * H]
         send(dw.at[kv, h, 1 - c], dwc.at[kv, h], s_dc, (kv, h), (kv, h), core)
 
+    def grad_near(kv, h, d, slot, e):
+        at = (kv, h, slot, e)
+        src, dst = dw.at[kv, h, c, ring_x(d), e], dwx.at[kv, h, slot, e]
+        send(src, dst, s_dx, at, at, at_x(ring_x(d)))
+
     def grad_core(kv, h):
         arrived(dwc.at[kv, h], s_dc, (kv, h))
         dw[kv, h, c] = (dw[kv, h, c].astype(f32) + dwc[kv, h].astype(f32)).astype(bf16)
-        for d in (1, 3, 2):
-            px = ring_x(d)
-            send(
-                dw.at[kv, h, c, px], dwx.at[kv, h, x], s_dx, (kv, h, px), (kv, h, x), at_x(px)
-            )
-
-    def grad_x(kv, h):
+        for d, e in ((1, 0), (3, 1)):
+            part = dw.at[kv, h, c, ring_x(2), e]
+            send(part, dwf.at[kv, h, e], s_df, (kv, h, e), (kv, h, e), at_x(ring_x(d)))
+        grad_near(kv, h, 1, 0, 1)
+        grad_near(kv, h, 3, 1, 0)
+
+    def grad_last(h):
+        arrived(dwc.at[0, h], s_dc, (0, h))
+        dw[0, h, c] = (dw[0, h, c].astype(f32) + dwc[0, h].astype(f32)).astype(bf16)
+        for d, slot in ((1, 0), (3, 1)):
+            for e in range(2):
+                grad_near(0, h, d, slot, e)
+        send(dw.at[0, h, c, ring_x(2)], dwd, s_df, (0, h, 0), (0, h, 0), at_x(ring_x(2)))
+
+    def grad_added(kv, h):
+        for d, slot in ((1, 0), (3, 1)):
+            arrived(dwf.at[kv, h, slot], s_df, (kv, h, slot))
+            mine = dw[kv, h, c, ring_x(d), slot].astype(f32)
+            total = mine + dwf[kv, h, slot].astype(f32)
+            dw[kv, h, c, ring_x(d), slot] = total.astype(bf16)
+            grad_near(kv, h, d, slot, slot)
+
+    def grad_x(kv, h, last=False):
         total = dw[kv, h, c, x].astype(f32)
-        for d in range(1, 4):
-            px = ring_x(d)
-            arrived(dwx.at[kv, h, px], s_dx, (kv, h, px))
-            total = total + dwx[kv, h, px].astype(f32)
+        if last:
+            arrived(dwd, s_df, (0, h, 0))
+            total = total + dwd[...].astype(f32)
+        for slot in range(2):
+            for e in range(2):
+                arrived(dwx.at[kv, h, slot, e], s_dx, (kv, h, slot, e))
+            total = total + dwx[kv, h, slot].astype(f32)
         zs[kv, h] = total.astype(bf16)
 
         def body(e):
@@ -425,28 +485,33 @@
 
     arrived(cot.at[1 - xh], s_cot, (0,))
 
-    def wait_partial(kv):
-        def body(d):
-            py = ring_y(d + 1)
-            arrived(precv.at[kv, py], s_p, (kv, py))
-
-        loop(3, body)
-
-    def summed(kv, t, s):
-        rows = pl.ds(pl.multiple_of(t * T, T), T)
-        cols = slice(s * H, (s + 1) * H)
-        total = own[kv, rows, cols]
+    def wait_partial(d):
+        py = ring_y(d + 1)
+        arrived(precv.at[0, py], s_p, (0, py))
+
+    def rows_cols(t, s):
+        return pl.ds(pl.multiple_of(t * T, T), T), slice(s * H, (s + 1) * H)
+
+    def key_sum(t, s):
+        rows, cols = rows_cols(t, s)
+        total = own[0, rows, cols]
         for d in range(1, 4):
-            total = total + precv[kv, ring_y(d), rows, cols].astype(f32)
+            total = total + precv[0, ring_y(d), rows, cols].astype(f32)
         return total
 
-    wait_partial(0)
+    def value_sum(t, s):
+        rows, cols = rows_cols(t, s)
+        near = precv[1, 0, rows, cols].astype(f32) + precv[1, 1, rows, cols].astype(f32)
+        return own[1, rows, cols] + near
+
+    loop(4, lambda i: w_on(1, i))
+    loop(3, wait_partial)
     hgain = hgain_ref[...].astype(f32)
     vx[x] = jnp.zeros((1, DC + H), f32)
 
     def key_block(t):
         for s in range(2):
-            key = summed(0, t, s)
+            key = key_sum(t, s)
             krinv = lax.rsqrt(jnp.mean(key * key, axis=-1, keepdims=True) + eps)
             kn = key * krinv
             oown[0, s, t] = (kn * hgain).astype(bf16)
@@ -467,29 +532,45 @@
         else:
             dhv[...] += part
 
+    loop(3, lambda i: grad_added(1, ring_y(i + lax.div(i, 2))))
     gather_far(1)
     grad_tile(1, ring_y(2))
     grad_tile(0, y)
+    loop(4, lambda i: w_core(1, i))
     back_panel(0, y, True)
     grad_core(1, ring_y(2))
     grad_core(0, y)
-    loop(4, lambda i: w_core(1, i))
+
+    def value_tile(i):
+        k = jnp.where(i == 0, 1, jnp.where(i == 1, 0, i))
+        h = ring_y(k + 1)
+        arrived(w.at[1, h, :, :, :, 1 - c], s_wc, (1, h))
+        forward(1, k)
+
+        @pl.when(i == 0)
+        def _():
+            far_send()
+
+        @pl.when(i == 1)
+        def _():
+            near_send(1, 0, 1)
+
+        @pl.when(i == 2)
+        def _():
+            near_send(3, 1, 0)
+
+    loop(3, value_tile)
     gather_near(0)
-
-    def value_tile(i):
-        h = ring_y(i + 1)
-        arrived(w.at[1, h, :, :, :, 1 - c], s_wc, (1, h))
-        forward(1, i)
-
-        @pl.when(i < 3)
-        def _():
-            partial_send(1, i + 1)
-
-    loop(4, value_tile)
+    value_tile(jnp.int32(3))
+    loop(3, lambda i: grad_x(1, ring_y(i + lax.div(i, 2))))
     loop(2, lambda i: grad_tile(0, ring_y(2 * i + 1)))
+    loop(2, lambda i: grad_core(0, ring_y(2 * i + 1)))
+    grad_added(1, ring_y(2))
+    grad_added(0, y)
     loop(4, lambda i: back_panel(1, i, False))
-    loop(2, lambda i: grad_core(0, ring_y(2 * i + 1)))
     loop(2, lambda i: back_panel(0, ring_y(2 * i + 1), False))
+    near_added()
+    loop(2, lambda i: grad_added(0, ring_y(2 * i + 1)))
     gather_far(0)
 
     def hidden_back(i):
@@ -513,8 +594,9 @@
         px = ring_x(d)
         send(vx.at[x], vx.at[x], s_vx, (px,), (x,), at_x(px))
     grad_tile(0, ring_y(2))
-
-    grad_core(0, ring_y(2))
+    grad_last(ring_y(2))
+    grad_x(1, ring_y(2))
+    grad_x(0, y)
 
     def vec_wait(ref, sems, me, n):
         def body(i):
@@ -523,7 +605,6 @@
 
         loop(n - 1, body)
 
-    loop(4, lambda i: grad_x(1, ring_y(i)))
     vec_wait(vx, s_vx, x, 4)
     vz[z] = (vx[0] + vx[1]) + (vx[2] + vx[3])
 
@@ -532,24 +613,26 @@
         send(vz.at[z], vz.at[z], s_vz, (pz,), (z,), at_z(pz))
 
     loop(7, vz_send)
-    grad_x(0, y)
     loop(2, lambda i: grad_x(0, ring_y(2 * i + 1)))
     grad_z(1)
+    grad_x(0, ring_y(2), True)
     vec_wait(vz, s_vz, z, 8)
     vc[c] = ((vz[0] + vz[1]) + (vz[2] + vz[3])) + ((vz[4] + vz[5]) + (vz[6] + vz[7]))
     send(vc.at[c], vc.at[c], s_vc, (0,), (0,), core)
-    grad_x(0, ring_y(2))
+    grad_z(0)
     arrived(vc.at[1 - c], s_vc, (0,))
     vy[y] = vc[0] + vc[1]
     for d in range(1, 4):
         py = ring_y(d)
         send(vy.at[y], vy.at[y], s_vy, (py,), (y,), at_y(py))
 
-    wait_partial(1)
+    for slot in range(2):
+        for half in range(2):
+            arrived(halves(precv.at[1, slot], half), s_pn, (slot, half))
 
     def value_block(t):
         for s in range(2):
-            oown[1, s, t] = summed(1, t, s).astype(bf16)
+            oown[1, s, t] = value_sum(t, s).astype(bf16)
 
     loop(4, value_block)
     send(oown.at[1, 1 - xh], orecv.at[1], s_out, (1,), (1,), opposite)
@@ -577,8 +660,6 @@
             ig_ref[rows, cols] = (rinv * (back - normed * mean)).astype(bf16)
 
     loop(8, input_rows)
-    grad_z(0)
-
     vec_wait(vy, s_vy, y, 4)
     for k in range(4):
         cols = slice(k * DC, (k + 1) * DC)
@@ -621,9 +702,6 @@
         sent(vx.at[x], s_vx, (px,))
         for kv in range(2):
             sent(w.at[kv, zh, xh, ze, xl, c, RA:R], s_wy, (kv, px))
-            for h in range(4):
-                sent(w.at[kv, h, xh, :, xl, c, 0:RA], s_wx, (kv, h, px))
-                sent(dw.at[kv, h, c, px], s_dx, (kv, h, px))
 
     loop(3, sent_x)
 
@@ -631,9 +709,24 @@
         for kv in range(2):
             sent(w.at[kv, h, :, :, :, c], s_wc, (kv, h))
             sent(dw.at[kv, h, 1 - c], s_dc, (kv, h))
+            for slot in range(2):
+                sent(of_x(kv, h, x), s_wx, (kv, h, slot))
+                sent(far_x(kv, h, x, slot), s_wx, (kv, h, 2 + slot))
+                if kv == 1:
+                    sent(dwf.at[kv, h, slot], s_df, (kv, h, slot))
+                for e in range(2):
+                    sent(dwx.at[kv, h, slot, e], s_dx, (kv, h, slot, e))
 
     loop(4, sent_core)
+    sent(dwd, s_df, (0, ring_y(2), 0))
+    for d in (0, 1, 3):
+        for slot in range(2):
+            sent(dwf.at[0, 0, slot], s_df, (0, ring_y(d), slot))
     sent(vc.at[c], s_vc, (0,))
+    for slot in range(2):
+        sent(pfar.at[slot], s_pf, (slot,))
+        for half in range(2):
+            sent(halves(precv.at[1, slot], half), s_pn, (slot, half))
     for kv in range(2):
         for slot in range(2):
             sent(cb.at[kv, y], s_ag, (kv, slot))
@@ -642,8 +735,7 @@
     def sent_y(i):
         py = ring_y(i + 1)
         sent(hid.at[py], s_hid, (py,))
-        for kv in range(2):
-            sent(psend.at[kv, py], s_p, (kv, py))
+        sent(psend.at[0, py], s_p, (0, py))
         sent(dhs.at[py], s_dh, (py,))
         sent(vy.at[y], s_vy, (py,))
 
@@ -676,6 +768,7 @@
         pltpu.VMEM((2, 4, 2, 2, 2, 2, R, H), bf16),
         pltpu.VMEM((2, 4, 4 * T, 2 * H), bf16),
         pltpu.VMEM((2, 4, 4 * T, 2 * H), bf16),
+        pltpu.VMEM((2, 2 * T, 2 * H), bf16),
         pltpu.VMEM((2, 4 * T, 2 * H), f32),
         pltpu.VMEM((2, 4, T, H), bf16),
         pltpu.VMEM((2, 4, 2, 4, T, H), bf16),
@@ -686,7 +779,9 @@
         pltpu.VMEM((4, T, DC), bf16),
         pltpu.VMEM((2, 4, 2, 4, 2, R, H), bf16),
         pltpu.VMEM((2, 4, 4, 2, R, H), bf16),
-        pltpu.VMEM((2, 4, 4, 2, R, H), bf16),
+        pltpu.VMEM((2, 4, 2, 2, R, H), bf16),
+        pltpu.VMEM((2, 4, 2, R, H), bf16),
+        pltpu.VMEM((2, R, H), bf16),
         pltpu.VMEM((2, 4, 2, R, H), bf16),
         pltpu.VMEM((2, 8, R, H), bf16),
         pltpu.VMEM((2, R, H), f32),
@@ -709,9 +804,12 @@
         sems(2, 4),
         sems(2, 4),
         sems(2),
+        sems(2, 2),
+        sems(2),
         sems(4),
         sems(2, 4),
-        sems(2, 4, 4),
+        sems(2, 4, 2, 2),
+        sems(2, 4, 2),
         sems(2, 8),
         sems(2),
         sems(4),

time: 107 us -> 102 us (0.953)
  Pallas kernels: 106 us -> 102 us
    pallas_call x1, Pallas kernels: 104 us -> 98.9 us  [on_device(): pl.pallas_call(kernel, out_shape=outs, in_specs=[anywhere, vmem, vmem, vm...]
where the time goes in v3:
time: 102 us
  Pallas kernels  102 us (100%)
    pallas_call x1, Pallas kernels, on_device(): pl.pallas_call(kernel, out_shape=outs, in_specs=[anywhere, vmem, vmem, vm...  98.9 us
    pallas_call x1, Pallas kernels, on_device(): pl.pallas_call(hand_out, out_shape=outs, in_specs=[pl.BlockSpec(memory_sp...  2.71 us

profile of v3, /device:TPU:16, one launch (start us, length us, event | category | flops | bytes accessed | tf_op | source)
XLA Modules:
  0.0 102.2 jit_solution(18406649735142263158)
XLA Ops:
  0.6 98.9 %shard_map.126 = (bf16[4,2,128,128]{3,2,1,0:T(8,128)(2,1)}, bf16[4,2,128,128]{3,2,1,0:T(8,128)(2,1)}, bf16[128,5120]{1,0:T(8,128)(2,1)}, f32[160,128]{1,0:T(8,12...) custom-call(bf16[128,5120]{1,0:T(8,128)(2,1)} %x_hbm.1, bf16[40,128]{1,0:T(8,128)(2,1)} %bitcast.13, ...), custom_call_target="tpu_custom_call" | custom-call | flops 8053063680 | bytes 6291456 | tf_op jit(solution)/shard_map/pallas_call | solution.py:832
  99.5 2.7 %shard_map.127 = (bf16[4,2,128,128]{3,2,1,0:T(8,128)(2,1)}, bf16[4,2,128,128]{3,2,1,0:T(8,128)(2,1)}, bf16[128,5120]{1,0:T(8,128)(2,1)}, f32[160,128]{1,0:T(8,12...) custom-call(bf16[4,2,128,128]{3,2,1,0:T(8,128)(2,1)} %get-tuple-element.21.refs_0_, ...), custom_call_target="tpu_custom_call" | custom-call | tf_op jit(solution)/shard_map/pallas_call | solution.py:853

commit v4 on v3

--- a/solution.py
+++ b/solution.py
@@ -41,13 +41,13 @@
     hgain_ref,
     kcot_ref,
     vcot_ref,
-    ks_ref,
-    vs_ref,
-    ig_ref,
-    dwk_ref,
-    dwv_ref,
-    ng_ref,
-    hg_ref,
+    ks_hbm,
+    vs_hbm,
+    ig_hbm,
+    dwk_hbm,
+    dwv_hbm,
+    ng_hbm,
+    hg_hbm,
     hid,
     hc,
     hct,
@@ -79,6 +79,9 @@
     rinv_s,
     gain_s,
     x_ref,
+    ig_ref,
+    ng_ref,
+    hg_ref,
     s_w0,
     s_wz,
     s_wx,
@@ -103,6 +106,8 @@
     s_vc,
     s_vy,
     s_in,
+    s_send,
+    s_res,
 ):
     dp, tn = lax.axis_index("dp"), lax.axis_index("tensor")
     z, xl, c = lax.div(dp, 4), lax.rem(lax.div(dp, 2), 2), lax.rem(dp, 2)
@@ -136,12 +141,41 @@
     partner = device(x, zh, 2 * y + ze, c)
     moved = zh != y
 
-    def send(src, dst, sems, s_at, r_at, to):
+    kinds = [
+        s_w0,
+        s_wz,
+        s_wx,
+        s_wy,
+        s_wr,
+        s_wc,
+        s_hid,
+        s_cot,
+        s_ag,
+        s_p,
+        s_pf,
+        s_pn,
+        s_out,
+        s_dh,
+        s_dc,
+        s_dx,
+        s_df,
+        s_dz,
+        s_dp,
+        s_vx,
+        s_vz,
+        s_vc,
+        s_vy,
+    ]
+
+    def kind(sems):
+        return next(i for i, known in enumerate(kinds) if known is sems)
+
+    def send(src, dst, sems, at, to):
         pltpu.make_async_remote_copy(
             src_ref=src,
             dst_ref=dst,
-            send_sem=sems.at[(0,) + s_at],
-            recv_sem=sems.at[(1,) + r_at],
+            send_sem=s_send.at[kind(sems)],
+            recv_sem=sems.at[at],
             device_id=to,
             device_id_type=MESH,
         ).start()
@@ -150,8 +184,8 @@
         return pltpu.make_async_remote_copy(
             src_ref=ref,
             dst_ref=ref,
-            send_sem=sems.at[(0,) + at],
-            recv_sem=sems.at[(1,) + at],
+            send_sem=s_send.at[kind(sems)],
+            recv_sem=sems.at[at],
             device_id=core,
             device_id_type=MESH,
         )
@@ -161,6 +195,13 @@
 
     def sent(ref, sems, at):
         copy_of(ref, sems, at).wait_send()
+
+    results = []
+
+    def hand_on(src, dst):
+        copy = pltpu.make_async_copy(src, dst, s_res.at[len(results)])
+        copy.start()
+        results.append(copy)
 
     barrier = pltpu.get_barrier_semaphore()
 
@@ -202,10 +243,10 @@
         @pl.when(moved)
         def _():
             ref = (wk_ref, wv_ref)[kv]
-            send(ref, w.at[kv, y, xh, ze, xl, c], s_w0, (kv,), (kv,), partner)
+            send(ref, w.at[kv, y, xh, ze, xl, c], s_w0, (kv,), partner)
 
     w_move(0)
-    send(vcot_ref.at[:, 1 - xh], cb.at[1, y, xh], s_cot, (1,), (1,), opposite)
+    send(vcot_ref.at[:, 1 - xh], cb.at[1, y, xh], s_cot, (1,), opposite)
 
     def norm_rows(i):
         rows = pl.ds(pl.multiple_of(i * 16, 16), 16)
@@ -220,7 +261,7 @@
     loop(8, norm_rows)
     for d in (1, 3, 2):
         py = ring_y(d)
-        send(hid.at[py], hc.at[y], s_hid, (py,), (y,), at_y(py))
+        send(hid.at[py], hc.at[y], s_hid, (0,), at_y(py))
     hc[y] = hid[y]
     local[1].wait()
     local[2].wait()
@@ -237,24 +278,21 @@
 
         def z_send(i):
             pz = ring_z(i + 1)
-            send(part, part, s_wz, (kv, pz), (kv, z), at_z(pz))
+            send(part, part, s_wz, (kv, z), at_z(pz))
 
         loop(7, z_send)
         rest = w.at[kv, zh, xh, ze, xl, c, RA:R]
         for d in (1, 3, 2):
             px = ring_x(d)
-            send(rest, rest, s_wy, (kv, px), (kv, x), at_x(px))
+            send(rest, rest, s_wy, (kv,), at_x(px))
 
     def w_second(kv):
-        for d in range(1, 4):
-            px = ring_x(d)
-            pxl, pxh = lax.rem(px, 2), lax.div(px, 2)
-            arrived(w.at[kv, zh, pxh, ze, pxl, c, RA:R], s_wy, (kv, px))
+        arrived(zr.at[kv, 0:3, 0 : R - RA], s_wy, (kv,))
         part = w.at[kv, zh, :, ze, :, c, RA:R]
 
         def z_send(i):
             pz = ring_z(i + 1)
-            send(part, part, s_wr, (kv, pz), (kv, z), at_z(pz))
+            send(part, part, s_wr, (kv, z), at_z(pz))
 
         loop(7, z_send)
 
@@ -270,27 +308,22 @@
 
         loop(2, wait_z)
         part = w.at[kv, h, xh, :, xl, c, 0:RA]
-        for d, slot in ((1, 0), (3, 1)):
-            send(part, part, s_wx, (kv, h, slot), (kv, h, slot), at_x(ring_x(d)))
-
-    def of_x(kv, h, px):
-        return w.at[kv, h, lax.div(px, 2), :, lax.rem(px, 2), c, 0:RA]
+        for d in (1, 3):
+            send(part, part, s_wx, (kv, h, 0), at_x(ring_x(d)))
 
     def far_x(kv, h, px, e):
         return w.at[kv, h, lax.div(px, 2), e, lax.rem(px, 2), c, 0:RA]
 
     def w_on(kv, i):
         h = ring_y(i + 1)
-        for d, slot in ((3, 0), (1, 1)):
-            arrived(of_x(kv, h, ring_x(d)), s_wx, (kv, h, slot))
+        arrived(w.at[kv, h, 0, :, :, c, 0:RA], s_wx, (kv, h, 0))
         for d, to, e in ((3, 1, 0), (1, 3, 1)):
             part = far_x(kv, h, ring_x(d), e)
-            send(part, part, s_wx, (kv, h, 2 + e), (kv, h, 2 + e), at_x(ring_x(to)))
+            send(part, part, s_wx, (kv, h, 1), at_x(ring_x(to)))
 
     def w_core(kv, i):
         h = ring_y(i + 1)
-        for e in range(2):
-            arrived(far_x(kv, h, ring_x(2), e), s_wx, (kv, h, 2 + e))
+        arrived(w.at[kv, h, 0, 0, :, c, 0:RA], s_wx, (kv, h, 1))
 
         def wait_z(e):
             pz = 2 * h + e
@@ -301,7 +334,7 @@
 
         loop(2, wait_z)
         part = w.at[kv, h, :, :, :, c]
-        send(part, part, s_wc, (kv, h), (kv, h), core)
+        send(part, part, s_wc, (kv, h), core)
 
     w_first(0)
     w_move(1)
@@ -309,7 +342,7 @@
     w_second(0)
     w_first(1)
     loop(4, lambda i: w_on(0, i))
-    send(kcot_ref.at[:, 1 - xh], cot.at[xh], s_cot, (0,), (0,), opposite)
+    send(kcot_ref.at[:, 1 - xh], cot.at[xh], s_cot, (0,), opposite)
 
     def panel(kv, h):
         return jnp.concatenate(
@@ -330,7 +363,7 @@
 
     def partial_send(kv, d):
         py = ring_y(d)
-        send(psend.at[kv, py], precv.at[kv, y], s_p, (kv, py), (kv, y), at_y(py))
+        send(psend.at[kv, py], precv.at[kv, y], s_p, (0,), at_y(py))
 
     def halves(ref, half):
         return ref.at[half * 2 * T : (half + 1) * 2 * T]
@@ -338,41 +371,35 @@
     def far_send():
         for d, half in ((1, 0), (3, 1)):
             part = halves(psend.at[1, ring_y(2)], half)
-            send(part, pfar.at[half], s_pf, (half,), (half,), at_y(ring_y(d)))
+            send(part, pfar.at[half], s_pf, (0,), at_y(ring_y(d)))
 
     def near_send(d, slot, half):
         src = halves(psend.at[1, ring_y(d)], half)
         dst = halves(precv.at[1, slot], half)
-        send(src, dst, s_pn, (slot, half), (slot, half), at_y(ring_y(d)))
+        send(src, dst, s_pn, (0,), at_y(ring_y(d)))
 
     def near_added():
+        arrived(pfar, s_pf, (0,))
         for d, slot in ((1, 0), (3, 1)):
-            arrived(pfar.at[slot], s_pf, (slot,))
             rows = slice(slot * 2 * T, (slot + 1) * 2 * T)
             total = psend[1, ring_y(d), rows].astype(f32) + pfar[slot].astype(f32)
             psend[1, ring_y(d), rows] = total.astype(bf16)
             near_send(d, slot, slot)
 
-    def hidden_wait(d):
-        py = ring_y(d + 1)
-        arrived(hc.at[py], s_hid, (py,))
-
-    loop(3, hidden_wait)
+    arrived(hc.at[0:3], s_hid, (0,))
 
     def gather(kv):
-        for d, slot in ((1, 0), (3, 1)):
-            send(cb.at[kv, y], cb.at[kv, y], s_ag, (kv, slot), (kv, slot), at_y(ring_y(d)))
+        for d in (1, 3):
+            send(cb.at[kv, y], cb.at[kv, y], s_ag, (kv, 0), at_y(ring_y(d)))
 
     def gather_near(kv):
-        for d, slot in ((3, 0), (1, 1)):
-            arrived(cb.at[kv, ring_y(d)], s_ag, (kv, slot))
-        for d, to, half, slot in ((3, 1, 0, 2), (1, 3, 2, 3)):
+        arrived(cb.at[kv, 0:2], s_ag, (kv, 0))
+        for d, to, half in ((3, 1, 0), (1, 3, 2)):
             part = cb.at[kv, ring_y(d), :, half : half + 2]
-            send(part, part, s_ag, (kv, slot), (kv, slot), at_y(ring_y(to)))
+            send(part, part, s_ag, (kv, 1), at_y(ring_y(to)))
 
     def gather_far(kv):
-        for half, slot in ((0, 2), (2, 3)):
-            arrived(cb.at[kv, ring_y(2), :, half : half + 2], s_ag, (kv, slot))
+        arrived(cb.at[kv, 0], s_ag, (kv, 1))
 
     arrived(cb.at[1, y, 1 - xh], s_cot, (1,))
     gather(1)
@@ -412,19 +439,18 @@
             for ph in range(2):
                 for pxl in range(2):
                     dw[kv, h, pc, 2 * ph + pxl] = g[:, pxl, pc, :, ph * H : (ph + 1) * H]
-        send(dw.at[kv, h, 1 - c], dwc.at[kv, h], s_dc, (kv, h), (kv, h), core)
+        send(dw.at[kv, h, 1 - c], dwc.at[kv, h], s_dc, (kv, h), core)
 
     def grad_near(kv, h, d, slot, e):
-        at = (kv, h, slot, e)
         src, dst = dw.at[kv, h, c, ring_x(d), e], dwx.at[kv, h, slot, e]
-        send(src, dst, s_dx, at, at, at_x(ring_x(d)))
+        send(src, dst, s_dx, (kv, h), at_x(ring_x(d)))
 
     def grad_core(kv, h):
         arrived(dwc.at[kv, h], s_dc, (kv, h))
         dw[kv, h, c] = (dw[kv, h, c].astype(f32) + dwc[kv, h].astype(f32)).astype(bf16)
         for d, e in ((1, 0), (3, 1)):
             part = dw.at[kv, h, c, ring_x(2), e]
-            send(part, dwf.at[kv, h, e], s_df, (kv, h, e), (kv, h, e), at_x(ring_x(d)))
+            send(part, dwf.at[kv, h, e], s_df, (kv, h), at_x(ring_x(d)))
         grad_near(kv, h, 1, 0, 1)
         grad_near(kv, h, 3, 1, 0)
 
@@ -434,11 +460,11 @@
         for d, slot in ((1, 0), (3, 1)):
             for e in range(2):
                 grad_near(0, h, d, slot, e)
-        send(dw.at[0, h, c, ring_x(2)], dwd, s_df, (0, h, 0), (0, h, 0), at_x(ring_x(2)))
+        send(dw.at[0, h, c, ring_x(2)], dwd, s_df, (0, h), at_x(ring_x(2)))
 
     def grad_added(kv, h):
+        arrived(dwf.at[kv, h], s_df, (kv, h))
         for d, slot in ((1, 0), (3, 1)):
-            arrived(dwf.at[kv, h, slot], s_df, (kv, h, slot))
             mine = dw[kv, h, c, ring_x(d), slot].astype(f32)
             total = mine + dwf[kv, h, slot].astype(f32)
             dw[kv, h, c, ring_x(d), slot] = total.astype(bf16)
@@ -447,11 +473,10 @@
     def grad_x(kv, h, last=False):
         total = dw[kv, h, c, x].astype(f32)
         if last:
-            arrived(dwd, s_df, (0, h, 0))
+            arrived(dwd, s_df, (0, h))
             total = total + dwd[...].astype(f32)
+        arrived(dwx.at[kv, h], s_dx, (kv, h))
         for slot in range(2):
-            for e in range(2):
-                arrived(dwx.at[kv, h, slot, e], s_dx, (kv, h, slot, e))
             total = total + dwx[kv, h, slot].astype(f32)
         zs[kv, h] = total.astype(bf16)
 
@@ -460,21 +485,21 @@
 
             @pl.when(pz != z)
             def _():
-                send(zs.at[kv, h, e], zr.at[kv, z], s_dz, (kv, pz), (kv, z), at_z(pz))
+                send(zs.at[kv, h, e], zr.at[kv, z], s_dz, (kv,), at_z(pz))
 
         loop(2, body)
 
     def grad_z(kv):
         total = zs[kv, zh, ze].astype(f32)
+        arrived(zr.at[kv, 0:7], s_dz, (kv,))
         for d in range(1, 8):
             pz = ring_z(d)
-            arrived(zr.at[kv, pz], s_dz, (kv, pz))
             total = total + zr[kv, pz].astype(f32)
 
         @pl.when(moved)
         def _():
             fin[kv] = total
-            send(fin.at[kv], finr.at[kv], s_dp, (kv,), (kv,), partner)
+            send(fin.at[kv], finr.at[kv], s_dp, (kv,), partner)
 
         @pl.when(jnp.logical_not(moved))
         def _():
@@ -484,10 +509,6 @@
     loop(3, lambda i: grad_core(1, ring_y(i + lax.div(i, 2))))
 
     arrived(cot.at[1 - xh], s_cot, (0,))
-
-    def wait_partial(d):
-        py = ring_y(d + 1)
-        arrived(precv.at[0, py], s_p, (0, py))
 
     def rows_cols(t, s):
         return pl.ds(pl.multiple_of(t * T, T), T), slice(s * H, (s + 1) * H)
@@ -505,7 +526,7 @@
         return own[1, rows, cols] + near
 
     loop(4, lambda i: w_on(1, i))
-    loop(3, wait_partial)
+    arrived(precv.at[0, 0:3], s_p, (0,))
     hgain = hgain_ref[...].astype(f32)
     vx[x] = jnp.zeros((1, DC + H), f32)
 
@@ -523,7 +544,8 @@
 
     loop(4, key_block)
     gather(0)
-    send(oown.at[0, 1 - xh], orecv.at[0], s_out, (0,), (0,), opposite)
+    send(oown.at[0, 1 - xh], orecv.at[0], s_out, (0,), opposite)
+    hand_on(oown.at[0, xh], ks_hbm.at[:, xh])
 
     def back_panel(kv, h, first):
         part = dot_nt(cots(kv, h), panel(kv, h)).reshape(4, T, DC)
@@ -583,7 +605,7 @@
         @pl.when(t != y)
         def _():
             dhs[t] = total.astype(bf16)
-            send(dhs.at[t], dhr.at[y], s_dh, (t,), (y,), at_y(t))
+            send(dhs.at[t], dhr.at[y], s_dh, (0,), at_y(t))
 
         @pl.when(t == y)
         def _():
@@ -592,56 +614,44 @@
     loop(4, hidden_back)
     for d in range(1, 4):
         px = ring_x(d)
-        send(vx.at[x], vx.at[x], s_vx, (px,), (x,), at_x(px))
+        send(vx.at[x], vx.at[x], s_vx, (0,), at_x(px))
     grad_tile(0, ring_y(2))
     grad_last(ring_y(2))
     grad_x(1, ring_y(2))
     grad_x(0, y)
 
-    def vec_wait(ref, sems, me, n):
-        def body(i):
-            p = lax.rem(me + 1 + i, n)
-            arrived(ref.at[p], sems, (p,))
-
-        loop(n - 1, body)
-
-    vec_wait(vx, s_vx, x, 4)
+    arrived(vx.at[0:3], s_vx, (0,))
     vz[z] = (vx[0] + vx[1]) + (vx[2] + vx[3])
 
     def vz_send(i):
         pz = ring_z(i + 1)
-        send(vz.at[z], vz.at[z], s_vz, (pz,), (z,), at_z(pz))
+        send(vz.at[z], vz.at[z], s_vz, (0,), at_z(pz))
 
     loop(7, vz_send)
     loop(2, lambda i: grad_x(0, ring_y(2 * i + 1)))
     grad_z(1)
     grad_x(0, ring_y(2), True)
-    vec_wait(vz, s_vz, z, 8)
+    arrived(vz.at[0:7], s_vz, (0,))
     vc[c] = ((vz[0] + vz[1]) + (vz[2] + vz[3])) + ((vz[4] + vz[5]) + (vz[6] + vz[7]))
-    send(vc.at[c], vc.at[c], s_vc, (0,), (0,), core)
+    send(vc.at[c], vc.at[c], s_vc, (0,), core)
     grad_z(0)
     arrived(vc.at[1 - c], s_vc, (0,))
     vy[y] = vc[0] + vc[1]
     for d in range(1, 4):
         py = ring_y(d)
-        send(vy.at[y], vy.at[y], s_vy, (py,), (y,), at_y(py))
-
-    for slot in range(2):
-        for half in range(2):
-            arrived(halves(precv.at[1, slot], half), s_pn, (slot, half))
+        send(vy.at[y], vy.at[y], s_vy, (0,), at_y(py))
+
+    arrived(precv.at[1, 0:2], s_pn, (0,))
 
     def value_block(t):
         for s in range(2):
             oown[1, s, t] = value_sum(t, s).astype(bf16)
 
     loop(4, value_block)
-    send(oown.at[1, 1 - xh], orecv.at[1], s_out, (1,), (1,), opposite)
-
-    def dh_wait(d):
-        py = ring_y(d + 1)
-        arrived(dhr.at[py], s_dh, (py,))
-
-    loop(3, dh_wait)
+    send(oown.at[1, 1 - xh], orecv.at[1], s_out, (1,), opposite)
+    hand_on(oown.at[1, xh], vs_hbm.at[:, xh])
+
+    arrived(dhr.at[0:3], s_dh, (0,))
 
     def input_rows(i):
         rows = pl.ds(pl.multiple_of(i * 16, 16), 16)
@@ -660,86 +670,53 @@
             ig_ref[rows, cols] = (rinv * (back - normed * mean)).astype(bf16)
 
     loop(8, input_rows)
-    vec_wait(vy, s_vy, y, 4)
+    hand_on(ig_ref, ig_hbm)
+    arrived(vy.at[0:3], s_vy, (0,))
     for k in range(4):
         cols = slice(k * DC, (k + 1) * DC)
         ng_ref[:, cols] = vy[k, :, :DC] / gain_s[:, cols]
     hg_ref[...] = (vy[0, :, DC:] + vy[1, :, DC:]) + (vy[2, :, DC:] + vy[3, :, DC:])
-    for kv, ref in ((0, ks_ref), (1, vs_ref)):
+    hand_on(ng_ref, ng_hbm)
+    hand_on(hg_ref, hg_hbm)
+    for kv, ref in ((0, ks_hbm), (1, vs_hbm)):
         arrived(orecv.at[kv], s_out, (kv,))
-        ref[:, xh] = oown[kv, xh]
-        ref[:, 1 - xh] = orecv[kv]
-    for kv, ref in ((0, dwk_ref), (1, dwv_ref)):
+        hand_on(orecv.at[kv], ref.at[:, 1 - xh])
+    for kv, ref in ((1, dwv_hbm), (0, dwk_hbm)):
 
         @pl.when(moved)
         def _():
             arrived(finr.at[kv], s_dp, (kv,))
 
-        ref[...] = finr[kv]
+        hand_on(finr.at[kv], ref)
 
     @pl.when(moved)
     def _():
-        for kv, ref in ((0, wk_ref), (1, wv_ref)):
-            sent(ref, s_w0, (kv,))
-            sent(fin.at[kv], s_dp, (kv,))
-
-    for kv, ref in ((0, kcot_ref), (1, vcot_ref)):
-        sent(ref.at[:, 1 - xh], s_cot, (kv,))
-        sent(oown.at[kv, 1 - xh], s_out, (kv,))
-
-    def sent_z(i):
-        pz = ring_z(i + 1)
-        for kv in range(2):
-            sent(w.at[kv, zh, xh, ze, xl, c, 0:RA], s_wz, (kv, pz))
-            sent(w.at[kv, zh, :, ze, :, c, RA:R], s_wr, (kv, pz))
-            sent(zs.at[kv, lax.div(pz, 2), lax.rem(pz, 2)], s_dz, (kv, pz))
-        sent(vz.at[z], s_vz, (pz,))
-
-    loop(7, sent_z)
-
-    def sent_x(i):
-        px = ring_x(i + 1)
-        sent(vx.at[x], s_vx, (px,))
-        for kv in range(2):
-            sent(w.at[kv, zh, xh, ze, xl, c, RA:R], s_wy, (kv, px))
-
-    loop(3, sent_x)
-
-    def sent_core(h):
-        for kv in range(2):
-            sent(w.at[kv, h, :, :, :, c], s_wc, (kv, h))
-            sent(dw.at[kv, h, 1 - c], s_dc, (kv, h))
-            for slot in range(2):
-                sent(of_x(kv, h, x), s_wx, (kv, h, slot))
-                sent(far_x(kv, h, x, slot), s_wx, (kv, h, 2 + slot))
-                if kv == 1:
-                    sent(dwf.at[kv, h, slot], s_df, (kv, h, slot))
-                for e in range(2):
-                    sent(dwx.at[kv, h, slot, e], s_dx, (kv, h, slot, e))
-
-    loop(4, sent_core)
-    sent(dwd, s_df, (0, ring_y(2), 0))
-    for d in (0, 1, 3):
-        for slot in range(2):
-            sent(dwf.at[0, 0, slot], s_df, (0, ring_y(d), slot))
-    sent(vc.at[c], s_vc, (0,))
-    for slot in range(2):
-        sent(pfar.at[slot], s_pf, (slot,))
-        for half in range(2):
-            sent(halves(precv.at[1, slot], half), s_pn, (slot, half))
-    for kv in range(2):
-        for slot in range(2):
-            sent(cb.at[kv, y], s_ag, (kv, slot))
-            sent(cb.at[kv, y, :, 0:2], s_ag, (kv, slot + 2))
-
-    def sent_y(i):
-        py = ring_y(i + 1)
-        sent(hid.at[py], s_hid, (py,))
-        sent(psend.at[0, py], s_p, (0, py))
-        sent(dhs.at[py], s_dh, (py,))
-        sent(vy.at[y], s_vy, (py,))
-
-    loop(3, sent_y)
+        sent(w.at[0, 0, 0, 0, 0], s_w0, (0,))
+        sent(fin, s_dp, (0,))
+
+    sent(zr.at[:, 0:7, 0:RA], s_wz, (0, 0))
+    sent(psend.at[:, :, 0 : 3 * RA], s_wx, (0, 0, 0))
+    sent(zr.at[:, 0:3, 0 : R - RA], s_wy, (0,))
+    sent(psend.at[0, :, 0 : 7 * (R - RA)], s_wr, (0, 0))
+    sent(w.at[:, :, :, :, :, 0], s_wc, (0, 0))
+    sent(hid.at[0:3], s_hid, (0,))
+    sent(cot, s_cot, (0,))
+    sent(cb.at[:, 0:3], s_ag, (0, 0))
+    sent(psend.at[0, 0:3], s_p, (0,))
+    sent(pfar, s_pf, (0,))
+    sent(precv.at[1, 0:2], s_pn, (0,))
+    sent(orecv, s_out, (0,))
+    sent(dhs.at[0:3], s_dh, (0,))
+    sent(dwc, s_dc, (0, 0))
+    sent(dwx, s_dx, (0, 0))
+    sent(dwf, s_df, (0, 0))
+    sent(zr.at[:, 0:7], s_dz, (0,))
+    sent(vx.at[0:3], s_vx, (0,))
+    sent(vz.at[0:7], s_vz, (0,))
+    sent(vc.at[0], s_vc, (0,))
+    sent(vy.at[0:3], s_vy, (0,))
+    for copy in results:
+        copy.wait()
 
 
 def hand_out(*refs):
@@ -759,7 +736,7 @@
     inputs, norm_gain, key_weight, value_weight, head_gain, key_cotangent, value_cotangent
 ):
     def sems(*shape):
-        return pltpu.SemaphoreType.DMA((2,) + shape)
+        return pltpu.SemaphoreType.DMA(shape)
 
     scratch = [
         pltpu.VMEM((4, T, DC), bf16),
@@ -793,30 +770,35 @@
         pltpu.VMEM((T, 128), f32),
         pltpu.VMEM((1, D), f32),
         pltpu.VMEM((T, D), bf16),
+        pltpu.VMEM((T, D), bf16),
+        pltpu.VMEM((1, D), f32),
+        pltpu.VMEM((1, H), f32),
         sems(2),
         sems(2, 8),
-        sems(2, 4, 4),
-        sems(2, 4),
+        sems(2, 4, 2),
+        sems(2),
         sems(2, 8),
         sems(2, 4),
-        sems(4),
+        sems(1),
         sems(2),
+        sems(2, 2),
+        sems(1),
+        sems(1),
+        sems(1),
+        sems(2),
+        sems(1),
+        sems(2, 4),
         sems(2, 4),
         sems(2, 4),
         sems(2),
-        sems(2, 2),
         sems(2),
-        sems(4),
-        sems(2, 4),
-        sems(2, 4, 2, 2),
-        sems(2, 4, 2),
-        sems(2, 8),
-        sems(2),
-        sems(4),
-        sems(8),
         sems(1),
-        sems(4),
-        pltpu.SemaphoreType.DMA((3,)),
+        sems(1),
+        sems(1),
+        sems(1),
+        sems(3),
+        sems(23),
+        sems(9),
     ]
     outs = (
         jax.ShapeDtypeStruct((4, 2, T, H), bf16),
@@ -833,7 +815,7 @@
         kernel,
         out_shape=outs,
         in_specs=[anywhere, vmem, vmem, vmem, vmem, anywhere, anywhere],
-        out_specs=(vmem,) * 7,
+        out_specs=(anywhere,) * 7,
         scratch_shapes=scratch,
         compiler_params=pltpu.CompilerParams(
             collective_id=0, has_side_effects=True, vmem_limit_bytes=60 * 1024 * 1024

time: 102 us -> 99.1 us (0.972)
  Pallas kernels: 102 us -> 97.8 us
    pallas_call x1, Pallas kernels: 98.9 us -> 95.1 us  [on_device(): pl.pallas_call(kernel, out_shape=outs, in_specs=[anywhere, vmem, vmem, vm...]
where the time goes in v4:
time: 99.1 us; the launch traced here: 98.5 us
  Pallas kernels  97.8 us (99%)
    pallas_call x1, Pallas kernels, on_device(): pl.pallas_call(kernel, out_shape=outs, in_specs=[anywhere, vmem, vmem, vm...  95.1 us
    pallas_call x1, Pallas kernels, on_device(): pl.pallas_call(hand_out, out_shape=outs, in_specs=[pl.BlockSpec(memory_sp...  2.71 us

profile of v4, /device:TPU:16, one launch (start us, length us, event | category | flops | bytes accessed | tf_op | source)
XLA Modules:
  0.0 98.5 jit_solution(4031255744492401099)
XLA Ops:
  0.6 95.1 %shard_map.126 = (bf16[4,2,128,128]{3,2,1,0:T(8,128)(2,1)}, bf16[4,2,128,128]{3,2,1,0:T(8,128)(2,1)}, bf16[128,5120]{1,0:T(8,128)(2,1)}, f32[160,128]{1,0:T(8,12...) custom-call(bf16[128,5120]{1,0:T(8,128)(2,1)} %x_hbm.1, bf16[40,128]{1,0:T(8,128)(2,1)} %bitcast.13, ...), custom_call_target="tpu_custom_call" | custom-call | flops 8053063680 | bytes 6291456 | tf_op jit(solution)/shard_map/pallas_call | solution.py:814
  95.8 2.7 %shard_map.127 = (bf16[4,2,128,128]{3,2,1,0:T(8,128)(2,1)}, bf16[4,2,128,128]{3,2,1,0:T(8,128)(2,1)}, bf16[128,5120]{1,0:T(8,128)(2,1)}, f32[160,128]{1,0:T(8,12...) custom-call(bf16[4,2,128,128]{3,2,1,0:T(8,128)(2,1)} %get-tuple-element.21.refs_0_, ...), custom_call_target="tpu_custom_call" | custom-call | tf_op jit(solution)/shard_map/pallas_call | solution.py:835

commit v5 on v4

--- a/solution.py
+++ b/solution.py
@@ -71,6 +71,7 @@
     zs,
     zr,
     fin,
+    finm,
     finr,
     vx,
     vz,
@@ -498,8 +499,8 @@
 
         @pl.when(moved)
         def _():
-            fin[kv] = total
-            send(fin.at[kv], finr.at[kv], s_dp, (kv,), partner)
+            fin[kv] = total.astype(bf16)
+            send(fin.at[kv], finm.at[kv], s_dp, (kv,), partner)
 
         @pl.when(jnp.logical_not(moved))
         def _():
@@ -611,11 +612,11 @@
         def _():
             dhr[y] = total.astype(bf16)
 
+    grad_tile(0, ring_y(2))
     loop(4, hidden_back)
     for d in range(1, 4):
         px = ring_x(d)
         send(vx.at[x], vx.at[x], s_vx, (0,), at_x(px))
-    grad_tile(0, ring_y(2))
     grad_last(ring_y(2))
     grad_x(1, ring_y(2))
     grad_x(0, y)
@@ -685,7 +686,8 @@
 
         @pl.when(moved)
         def _():
-            arrived(finr.at[kv], s_dp, (kv,))
+            arrived(finm.at[kv], s_dp, (kv,))
+            finr[kv] = finm[kv].astype(f32)
 
         hand_on(finr.at[kv], ref)
 
@@ -721,13 +723,22 @@
 
 def hand_out(*refs):
     ins, outs, held, sems = refs[:7], refs[7:14], refs[14:21], refs[21]
-    first = [pltpu.make_async_copy(ins[i], held[i], sems.at[0, i]) for i in range(7)]
-    last = [pltpu.make_async_copy(held[i], outs[i], sems.at[1, i]) for i in range(7)]
+    parts = [(2, k) for k in range(4)] + [(0, None), (1, None)]
+    parts += [(i, None) for i in range(3, 7)]
+
+    def view(ref, k):
+        return ref if k is None else ref.at[32 * k : 32 * k + 32]
+
+    first, last = [], []
+    for n, (i, k) in enumerate(parts):
+        src, mid, dst = view(ins[i], k), view(held[i], k), view(outs[i], k)
+        first.append(pltpu.make_async_copy(src, mid, sems.at[0, n]))
+        last.append(pltpu.make_async_copy(mid, dst, sems.at[1, n]))
     for copy in first:
         copy.start()
-    for i in range(7):
-        first[i].wait()
-        last[i].start()
+    for n in range(len(parts)):
+        first[n].wait()
+        last[n].start()
     for copy in last:
         copy.wait()
 
@@ -761,7 +772,8 @@
         pltpu.VMEM((2, R, H), bf16),
         pltpu.VMEM((2, 4, 2, R, H), bf16),
         pltpu.VMEM((2, 8, R, H), bf16),
-        pltpu.VMEM((2, R, H), f32),
+        pltpu.VMEM((2, R, H), bf16),
+        pltpu.VMEM((2, R, H), bf16),
         pltpu.VMEM((2, R, H), f32),
         pltpu.VMEM((4, 1, DC + H), f32),
         pltpu.VMEM((8, 1, DC + H), f32),
@@ -838,7 +850,7 @@
         in_specs=[pl.BlockSpec(memory_space=pl.ANY)] * 7,
         out_specs=(pl.BlockSpec(memory_space=pl.ANY),) * 7,
         scratch_shapes=[pltpu.VMEM(o.shape, o.dtype) for o in outs]
-        + [pltpu.SemaphoreType.DMA((2, 7))],
+        + [pltpu.SemaphoreType.DMA((2, 10))],
         compiler_params=pltpu.CompilerParams(vmem_limit_bytes=60 * 1024 * 1024),
     )(*results)
     return (

time: 99.1 us -> 95.6 us (0.965)
  Pallas kernels: 97.8 us -> 94.7 us
    pallas_call x1, Pallas kernels: 95.1 us -> 92.3 us  [on_device(): pl.pallas_call(kernel, out_shape=outs, in_specs=[anywhere, vmem, vmem, vm...]
where the time goes in v5:
time: 95.6 us; the launch traced here: 95.4 us
  Pallas kernels  94.7 us (99%)
    pallas_call x1, Pallas kernels, on_device(): pl.pallas_call(kernel, out_shape=outs, in_specs=[anywhere, vmem, vmem, vm...  92.3 us
    pallas_call x1, Pallas kernels, on_device(): pl.pallas_call(hand_out, out_shape=outs, in_specs=[pl.BlockSpec(memory_sp...  2.42 us

profile of v5, /device:TPU:16, one launch (start us, length us, event | category | flops | bytes accessed | tf_op | source)
XLA Modules:
  0.0 95.4 jit_solution(1470682746448513124)
XLA Ops:
  0.6 92.3 %shard_map.126 = (bf16[4,2,128,128]{3,2,1,0:T(8,128)(2,1)}, bf16[4,2,128,128]{3,2,1,0:T(8,128)(2,1)}, bf16[128,5120]{1,0:T(8,128)(2,1)}, f32[160,128]{1,0:T(8,12...) custom-call(bf16[128,5120]{1,0:T(8,128)(2,1)} %x_hbm.1, bf16[40,128]{1,0:T(8,128)(2,1)} %bitcast.13, ...), custom_call_target="tpu_custom_call" | custom-call | flops 8053063680 | bytes 6291456 | tf_op jit(solution)/shard_map/pallas_call | solution.py:826
  93.0 2.4 %shard_map.127 = (bf16[4,2,128,128]{3,2,1,0:T(8,128)(2,1)}, bf16[4,2,128,128]{3,2,1,0:T(8,128)(2,1)}, bf16[128,5120]{1,0:T(8,128)(2,1)}, f32[160,128]{1,0:T(8,12...) custom-call(bf16[4,2,128,128]{3,2,1,0:T(8,128)(2,1)} %get-tuple-element.21.refs_0_, ...), custom_call_target="tpu_custom_call" | custom-call | tf_op jit(solution)/shard_map/pallas_call | solution.py:847

commit v6 on v5

--- a/solution.py
+++ b/solution.py
@@ -556,11 +556,11 @@
             dhv[...] += part
 
     loop(3, lambda i: grad_added(1, ring_y(i + lax.div(i, 2))))
+    grad_tile(0, y)
+    back_panel(0, y, True)
     gather_far(1)
     grad_tile(1, ring_y(2))
-    grad_tile(0, y)
     loop(4, lambda i: w_core(1, i))
-    back_panel(0, y, True)
     grad_core(1, ring_y(2))
     grad_core(0, y)
 
@@ -593,7 +593,6 @@
     loop(4, lambda i: back_panel(1, i, False))
     loop(2, lambda i: back_panel(0, ring_y(2 * i + 1), False))
     near_added()
-    loop(2, lambda i: grad_added(0, ring_y(2 * i + 1)))
     gather_far(0)
 
     def hidden_back(i):
@@ -613,6 +612,7 @@
             dhr[y] = total.astype(bf16)
 
     grad_tile(0, ring_y(2))
+    loop(2, lambda i: grad_added(0, ring_y(2 * i + 1)))
     loop(4, hidden_back)
     for d in range(1, 4):
         px = ring_x(d)

time: 95.6 us -> 94.9 us (level)
  no operation moved by 1% of the time
where the time goes in v6:
time: 94.9 us; the launch traced here: 94.7 us
  Pallas kernels  94 us (99%)
    pallas_call x1, Pallas kernels, on_device(): pl.pallas_call(kernel, out_shape=outs, in_specs=[anywhere, vmem, vmem, vm...  91.6 us
    pallas_call x1, Pallas kernels, on_device(): pl.pallas_call(hand_out, out_shape=outs, in_specs=[pl.BlockSpec(memory_sp...  2.42 us

profile of v6, /device:TPU:16, one launch (start us, length us, event | category | flops | bytes accessed | tf_op | source)
XLA Modules:
  0.0 94.7 jit_solution(7407089999198351689)
XLA Ops:
  0.6 91.6 %shard_map.126 = (bf16[4,2,128,128]{3,2,1,0:T(8,128)(2,1)}, bf16[4,2,128,128]{3,2,1,0:T(8,128)(2,1)}, bf16[128,5120]{1,0:T(8,128)(2,1)}, f32[160,128]{1,0:T(8,12...) custom-call(bf16[128,5120]{1,0:T(8,128)(2,1)} %x_hbm.1, bf16[40,128]{1,0:T(8,128)(2,1)} %bitcast.13, ...), custom_call_target="tpu_custom_call" | custom-call | flops 8053063680 | bytes 6291456 | tf_op jit(solution)/shard_map/pallas_call | solution.py:826
  92.3 2.4 %shard_map.127 = (bf16[4,2,128,128]{3,2,1,0:T(8,128)(2,1)}, bf16[4,2,128,128]{3,2,1,0:T(8,128)(2,1)}, bf16[128,5120]{1,0:T(8,128)(2,1)}, f32[160,128]{1,0:T(8,12...) custom-call(bf16[4,2,128,128]{3,2,1,0:T(8,128)(2,1)} %get-tuple-element.21.refs_0_, ...), custom_call_target="tpu_custom_call" | custom-call | tf_op jit(solution)/shard_map/pallas_call | solution.py:847

commit v7 on v6

--- a/solution.py
+++ b/solution.py
@@ -227,8 +227,9 @@
     ]
     for copy in local:
         copy.start()
+    gains = gain_ref[...].astype(f32)
     for k in range(D // 128):
-        gain_s[:, k * 128 : (k + 1) * 128] = gain_ref[k : k + 1, :].astype(f32)
+        gain_s[:, k * 128 : (k + 1) * 128] = gains[k : k + 1, :]
 
     def w_own(kv):
         return w.at[kv, zh, xh, ze, xl, c]

time: 94.9 us -> 94.9 us (level)
  no operation moved by 1% of the time
where the time goes in v7:
time: 94.9 us; the launch traced here: 94.7 us
  Pallas kernels  94 us (99%)
    pallas_call x1, Pallas kernels, on_device(): pl.pallas_call(kernel, out_shape=outs, in_specs=[anywhere, vmem, vmem, vm...  91.6 us
    pallas_call x1, Pallas kernels, on_device(): pl.pallas_call(hand_out, out_shape=outs, in_specs=[pl.BlockSpec(memory_sp...  2.42 us

profile of v7, /device:TPU:16, one launch (start us, length us, event | category | flops | bytes accessed | tf_op | source)
XLA Modules:
  0.0 94.7 jit_solution(6084823302041960036)
XLA Ops:
  0.6 91.6 %shard_map.126 = (bf16[4,2,128,128]{3,2,1,0:T(8,128)(2,1)}, bf16[4,2,128,128]{3,2,1,0:T(8,128)(2,1)}, bf16[128,5120]{1,0:T(8,128)(2,1)}, f32[160,128]{1,0:T(8,12...) custom-call(bf16[128,5120]{1,0:T(8,128)(2,1)} %x_hbm.1, bf16[40,128]{1,0:T(8,128)(2,1)} %bitcast.13, ...), custom_call_target="tpu_custom_call" | custom-call | flops 8053063680 | bytes 6291456 | tf_op jit(solution)/shard_map/pallas_call | solution.py:827
  92.3 2.4 %shard_map.127 = (bf16[4,2,128,128]{3,2,1,0:T(8,128)(2,1)}, bf16[4,2,128,128]{3,2,1,0:T(8,128)(2,1)}, bf16[128,5120]{1,0:T(8,128)(2,1)}, f32[160,128]{1,0:T(8,12...) custom-call(bf16[4,2,128,128]{3,2,1,0:T(8,128)(2,1)} %get-tuple-element.21.refs_0_, ...), custom_call_target="tpu_custom_call" | custom-call | tf_op jit(solution)/shard_map/pallas_call | solution.py:848
